TPU v7x, 512 devices: a whole 4x4x16 slice. The times are simulated.
512 devices in a mesh: band: 4 (over x), group: 16 (over z), patch: 8 (over y, core).
Axes of the slice: x: 4, y: 4, z: 16, core: 2. Of those that a mesh axis runs over, the one named last changes fastest.
Arguments:
- tile_flux: bfloat16 [4, 1024, 128, 128], P('band', ('group', 'patch')), may hold values from -6 to 6
- inverse_var: bfloat16 [4, 1024, 128, 128], P('band', ('group', 'patch')), may hold values from 0.25 to 4
- kernel_coef: bfloat16 [4, 1024, 27], P('band', ('group', 'patch')), may hold values from -4 to 4
- owner_index: int32 [4, 1024, 1], P('band', ('group', 'patch')), may hold values from 0 to 7; in each aligned block of 8 rows (0 to 7, 8 to 15, ..., all dimensions but the last counted through in order) at most 2 rows name the same one
- offsets: int32 [4, 1024, 2], P('band', ('group', 'patch')), may hold values from 0 to 48
- pad_widths: int32 [4, 1024, 4], P('band', ('group', 'patch')), may hold values from 0 to 32
Outputs:
- coadd: float32 [4, 8, 512, 512], P('band', 'patch', 'group')
- chi_square: float32 [8, 512, 512], P('patch', 'group')
Inputs may be any that keep to these rules, and one draw needn't show every extreme that they name: `owner_index`: among the 8 tiles of one device (an aligned block of rows of a band), no patch is named more than 2 times, a bound that some block reaches.
All inputs are finite; a program needn't handle non-finite values.
Results may differ from a plain program's by a relative error of at most 0.0044.
Values may be sent and summed in bfloat16 or wider, within the bound.
No kernel may reach another device: no remote copies, remote signals or barrier semaphores. Data moves between devices by JAX's collectives and lax.ppermute only.
A program may use at most 64 MiB of HBM per device.

v0:
```python
import jax
import jax.numpy as jnp
import numpy as np
from jax import lax
from jax.sharding import PartitionSpec as P

PATCH_SIDE = 512


SPREADS = (0.7, 1.5, 3.0)
DEGREES = (4, 2, 2)
REACH = 10


def basis_filters():
    offsets_axis = np.arange(-REACH, REACH + 1) * 1.0
    filters = []
    for spread_value, degree in zip(SPREADS, DEGREES):
        profile = np.exp(-(offsets_axis**2) / (2.0 * spread_value * spread_value))
        profile = profile / profile.sum()
        for exponent in range(degree + 1):
            filters.append(profile * (offsets_axis / REACH) ** exponent)
    return np.stack(filters)


def term_table():
    starts = np.cumsum([0] + [degree + 1 for degree in DEGREES])
    filter_count = int(starts[-1])
    term_count = sum(((degree + 1) * (degree + 2) // 2 for degree in DEGREES))
    table = np.zeros((filter_count, filter_count, term_count))
    counter = 0
    for family, degree in enumerate(DEGREES):
        for along_x in range(degree + 1):
            for along_y in range(degree + 1 - along_x):
                table[starts[family] + along_x, starts[family] + along_y, counter] = 1.0
                counter += 1
    return table


def band_tables(tile_side):
    filters = basis_filters()
    source = np.arange(tile_side)[:, None]
    target = np.arange(tile_side)[None, :]
    shift_table = target - source
    inside = np.abs(shift_table) <= REACH
    picked = filters[:, np.clip(shift_table + REACH, 0, 2 * REACH)] * inside
    row_table = np.transpose(picked, (1, 0, 2))
    column_table = np.transpose(picked, (0, 2, 1))
    row_half = jnp.asarray(row_table, jnp.float32).astype(jnp.bfloat16)
    column_half = jnp.asarray(column_table, jnp.float32).astype(jnp.bfloat16)
    return (row_half, column_half, jnp.asarray(term_table(), jnp.float32))


def match_block(tile_block, coef_block, tables):
    row_half, column_half, expand = tables
    rowpass = jnp.einsum("nyz,zfx->nyfx", tile_block, row_half, preferred_element_type=jnp.float32)
    mixing = jnp.einsum(
        "nt,fgt->nfg", coef_block.astype(jnp.float32), expand, precision=lax.Precision.HIGHEST
    )
    mixed_half = jnp.einsum(
        "nyfx,nfg->nygx", rowpass, mixing, precision=lax.Precision.HIGHEST
    ).astype(jnp.bfloat16)
    return jnp.einsum("gyz,nzgx->nyx", column_half, mixed_half, preferred_element_type=jnp.float32)


def match_tiles(tile_block, coef_block):
    tables = band_tables(tile_block.shape[-1])
    tile_total = tile_block.shape[0]
    pieces = []
    for block_start in range(0, tile_total, 8):
        pieces.append(
            match_block(
                tile_block[block_start : block_start + 8],
                coef_block[block_start : block_start + 8],
                tables,
            )
        )
    return jnp.concatenate(pieces, axis=0)


def tile_mask(pad_values, tile_side):
    pixel_line = jnp.arange(tile_side, dtype=jnp.float32)[None, :]
    rows_ok = (pixel_line >= pad_values[:, 0:1]) & (pixel_line < tile_side - pad_values[:, 1:2])
    cols_ok = (pixel_line >= pad_values[:, 2:3]) & (pixel_line < tile_side - pad_values[:, 3:4])
    return (rows_ok[:, :, None] & cols_ok[:, None, :]).astype(jnp.float32)


def on_device(tile_flux, inverse_var, kernel_coef, owner_index, offsets, pad_widths):
    patch_count = lax.axis_size("patch")
    tile_count = tile_flux.shape[1]
    tile_side = tile_flux.shape[2]
    term_count = kernel_coef.shape[2]
    capacity = max(2 * tile_count // patch_count, 2)
    slot_total = patch_count * capacity
    target = owner_index[0, :, 0]
    tile_line = jnp.arange(tile_count)
    earlier = (target[None, :] == target[:, None]) & (tile_line[None, :] < tile_line[:, None])
    slot_rank = jnp.sum(earlier.astype(jnp.int32), axis=1)
    position = target * capacity + slot_rank
    placing = (jnp.arange(slot_total)[:, None] == position[None, :]).astype(jnp.float32)
    tile_meta = jnp.concatenate([offsets[0], pad_widths[0]], axis=1).astype(jnp.float32)
    packed_meta = jnp.dot(placing, tile_meta, precision=lax.Precision.HIGHEST)
    placing_half = placing.astype(jnp.bfloat16)
    packed_flux = jnp.einsum(
        "st,tyx->syx", placing_half, tile_flux[0], preferred_element_type=jnp.float32
    )
    packed_flux = packed_flux.astype(jnp.bfloat16).reshape(
        patch_count, capacity, tile_side, tile_side
    )
    packed_var = jnp.einsum(
        "st,tyx->syx", placing_half, inverse_var[0], preferred_element_type=jnp.float32
    )
    packed_var = packed_var.astype(jnp.bfloat16).reshape(
        patch_count, capacity, tile_side, tile_side
    )
    packed_coef = jnp.dot(placing_half, kernel_coef[0], preferred_element_type=jnp.float32)
    packed_coef = packed_coef.astype(jnp.bfloat16).reshape(patch_count, capacity, term_count)
    meta_half = packed_meta.astype(jnp.bfloat16).reshape(patch_count, capacity, 6)
    got_flux = lax.all_to_all(packed_flux, "patch", split_axis=0, concat_axis=0, tiled=True)
    got_var = lax.all_to_all(packed_var, "patch", split_axis=0, concat_axis=0, tiled=True)
    got_coef = lax.all_to_all(packed_coef, "patch", split_axis=0, concat_axis=0, tiled=True)
    got_meta = lax.all_to_all(meta_half, "patch", split_axis=0, concat_axis=0, tiled=True)
    leading = got_flux.shape[:2]
    flat_meta = got_meta.reshape(-1, 6).astype(jnp.float32)
    matched = match_tiles(
        got_flux.reshape(-1, tile_side, tile_side), got_coef.reshape(-1, term_count)
    )
    weight = got_var.reshape(-1, tile_side, tile_side).astype(jnp.float32) * tile_mask(
        flat_meta[:, 2:6], tile_side
    )
    weighted = (weight * matched).reshape(leading + (tile_side, tile_side))
    weight_got = weight.reshape(leading + (tile_side, tile_side))
    arrived = flat_meta.reshape(leading + (6,))
    weighted = weighted.reshape(-1, tile_side, tile_side)
    weight_got = weight_got.reshape(-1, tile_side, tile_side)
    corners = (arrived.reshape(-1, 6)[:, 0:2] * 8.0).astype(jnp.int32)

    def place(slot_index, totals):
        flux_sum, weight_sum = totals
        corner = (corners[slot_index, 0], corners[slot_index, 1])
        region = lax.dynamic_slice(flux_sum, corner, (tile_side, tile_side)) + weighted[slot_index]
        flux_sum = lax.dynamic_update_slice(flux_sum, region, corner)
        region = (
            lax.dynamic_slice(weight_sum, corner, (tile_side, tile_side)) + weight_got[slot_index]
        )
        weight_sum = lax.dynamic_update_slice(weight_sum, region, corner)
        return (flux_sum, weight_sum)

    empty = jnp.zeros((PATCH_SIDE, PATCH_SIDE), jnp.float32)
    flux_sum, weight_sum = lax.fori_loop(0, slot_total, place, (empty, empty))
    flux_total, weight_total = lax.psum((flux_sum, weight_sum), "group")
    share_rows = PATCH_SIDE // lax.axis_size("group")
    first_row = lax.axis_index("group") * share_rows
    flux_part = lax.dynamic_slice_in_dim(flux_total, first_row, share_rows, 0)
    weight_part = lax.dynamic_slice_in_dim(weight_total, first_row, share_rows, 0)
    denominator = weight_part + 1.0
    coadd = flux_part / denominator
    chi_local = flux_part * flux_part / denominator
    chi_total = lax.psum(chi_local, "band")
    return (coadd[None, None], chi_total[None])


def solution(mesh):
    return jax.shard_map(
        on_device,
        mesh=mesh,
        in_specs=(
            P("band", ("group", "patch"), None, None),
            P("band", ("group", "patch"), None, None),
            P("band", ("group", "patch"), None),
            P("band", ("group", "patch"), None),
            P("band", ("group", "patch"), None),
            P("band", ("group", "patch"), None),
        ),
        out_specs=(P("band", "patch", "group", None), P("patch", "group", None)),
        check_vma=False,
    )
```

profile of v0, /device:TPU:1, one launch (start us, length us, event | category | flops | bytes accessed | tf_op | source)
XLA Modules:
  0.0 452.4 jit_solution(7939290222382438091)
XLA Ops:
  10.3 10.1 %all-to-all-start = ((bf16[8,2,6]{2,1,0:T(2,128)(2,1)}), bf16[8,2,6]{2,1,0:T(2,128)(2,1)S(1)}, u32[]{:S(2)}, u32[]{:S(2)}) async-start(bf16[8,2,6]{2,1,0:T(2,128)(2,1)} %bitcast.7), calls=%async_computation | async-start | bytes 8192 | tf_op jit(solution)/shard_map/all_to_all | solution.py:122
  26.1 4.8 %all-to-all-start.2 = ((bf16[8,2,27]{2,1,0:T(2,128)(2,1)}), bf16[8,2,27]{2,1,0:T(2,128)(2,1)S(1)}, u32[]{:S(2)}, u32[]{:S(2)}) async-start(bf16[8,2,27]{2,1,0:T(2,128)(2,1)} %bitcast.15), calls=%async_computation.2 | async-start | bytes 8192 | tf_op jit(solution)/shard_map/all_to_all | solution.py:121
  31.4 4.1 all-to-all-done.2
  35.5 4.1 all-to-all-start.3
  42.2 6.9 %all-to-all-done.3 = bf16[8,2,128,128]{3,1,2,0:T(2,128)(2,1)S(1)} async-done(((bf16[8,2,128,128]{3,1,2,0:T(2,128)(2,1)}), bf16[8,2,128,128]{3,1,2,0:T(2,128)(2,1)S(1)}, u32[]{:S(2)}, u32[]{:S(2)}) %all-to-all-start.3) | async-done | bytes 524320 | tf_op jit(solution)/shard_map/all_to_all | solution.py:119
  49.1 4.3 all-to-all-start.1
  55.9 8.8 %convert_bitcast_fusion.1 = bf16[8,128,11,128]{3,2,1,0:T(8,128)(2,1)S(1)} fusion(f32[8,128,11,128]{3,0,2,1:T(8,128)S(1)} %fusion.40, f32[8,11,11,1]{2,0,1,3:T(8,128)S(1)} %convolution_bitcast_fusion.1), kind=kOutput, calls=%fused_computation.11 | convolution fusion | flops 191758336 | bytes 8654624 | tf_op jit(solution)/shard_map/nyfx,nfg->nygx/dot_general | solution.py:60
  64.7 8.6 %convert_bitcast_fusion = bf16[8,128,11,128]{3,2,1,0:T(8,128)(2,1)S(1)} fusion(f32[8,128,11,128]{3,0,2,1:T(8,128)S(1)} %fusion.41, f32[8,11,11,1]{2,0,1,3:T(8,128)S(1)} %convolution_bitcast_fusion), kind=kOutput, calls=%fused_computation.10 | convolution fusion | flops 191758336 | bytes 8654624 | tf_op jit(solution)/shard_map/nyfx,nfg->nygx/dot_general | solution.py:60
  77.6 160.3 %while.15 = (s32[]{:T(128)}, f32[512,512]{1,0:T(8,128)S(1)}, f32[512,512]{1,0:T(8,128)S(1)}, s32[16,2]{0,1:T(2,128)S(1)}, f32[16,128,128]{1,2,0:T(8,128)}, /*ind...) while((s32[]{:T(128)}, f32[512,512]{1,0:T(8,128)S(1)}, f32[512,512]{1,0:T(8,128)S(1)}, ...), condition=%wide.region_2.0_spmd, body=%wide.region_1.0_spmd.sunk | while | flops 32776 | bytes 1179853 | solution.py:150
  85.8 1.7 dynamic_update_slice.16
  95.7 1.7 dynamic_update_slice.16
  103.8 2.0 dynamic_update_slice.17
  105.9 2.0 dynamic_update_slice.16
  114.4 1.7 dynamic_update_slice.17
  124.3 2.0 dynamic_update_slice.17
  126.3 2.0 dynamic_update_slice.16
  136.5 1.7 dynamic_update_slice.16
  144.7 2.0 dynamic_update_slice.17
  146.7 2.0 dynamic_update_slice.16
  155.3 1.7 dynamic_update_slice.17
  157.0 1.7 dynamic_update_slice.16
  165.1 1.7 dynamic_update_slice.17
  166.8 1.7 dynamic_update_slice.16
  175.0 1.7 dynamic_update_slice.17
  184.9 2.0 dynamic_update_slice.17
  186.9 2.0 dynamic_update_slice.16
  195.5 1.7 dynamic_update_slice.17
  197.1 1.7 dynamic_update_slice.16
  214.9 1.7 dynamic_update_slice.17
  226.4 1.7 dynamic_update_slice.16
  239.3 142.6 %all-reduce.6.cloned.1.call-done = (f32[512,512]{1,0:T(8,128)}, f32[512,512]{1,0:T(8,128)}) async-done(((f32[512,512]{1,0:T(8,128)}, f32[512,512]{1,0:T(8,128)}), (f32[512,512]{1,0:T(8,128)}, f32[512,512]{1,0:T(8,128)})) %all-reduce.6.cloned.1.call-update) | async-done | bytes 2097168 | tf_op jit(solution)/shard_map/psum | solution.py:151
  383.5 60.6 %all-reduce.4.cloned.1.call-done = f32[1,32,512]{2,1,0:T(8,128)} async-done(((f32[1,32,512]{2,1,0:T(8,128)}), f32[1,32,512]{2,1,0:T(8,128)}) %all-reduce.4.cloned.1.call-update) | async-done | bytes 65552 | tf_op jit(solution)/shard_map/psum | solution.py:159
  (156 shorter events, 82.4 us)
Async XLA Ops:
  7.2 13.3 %copy-start = (bf16[1,8,128,128]{3,2,1,0:T(8,128)(2,1)S(1)}, bf16[1,8,128,128]{3,2,1,0:T(8,128)(2,1)}, u32[]{:S(2)}) copy-start(bf16[1,8,128,128]{3,2,1,0:T(8,128)(2,1)} %param.11) | copy-start | bytes 786436
  7.2 46.9 %copy-start.3 = (bf16[128,11,128,1]{2,0,1,3:T(8,128)(2,1)S(1)}, bf16[128,11,128,1]{2,0,1,3:T(8,128)(2,1)}, u32[]{:S(2)}) copy-start(bf16[128,11,128,1]{2,0,1,3:T(8,128)(2,1)} %constant.68) | copy-start | bytes 1081348
  10.3 15.8 %all-to-all-start = ((bf16[8,2,6]{2,1,0:T(2,128)(2,1)}), bf16[8,2,6]{2,1,0:T(2,128)(2,1)S(1)}, u32[]{:S(2)}, u32[]{:S(2)}) async-start(bf16[8,2,6]{2,1,0:T(2,128)(2,1)} %bitcast.7), calls=%async_computation | async-start | bytes 8192 | tf_op jit(solution)/shard_map/all_to_all | solution.py:122
  26.1 9.3 %all-to-all-start.2 = ((bf16[8,2,27]{2,1,0:T(2,128)(2,1)}), bf16[8,2,27]{2,1,0:T(2,128)(2,1)S(1)}, u32[]{:S(2)}, u32[]{:S(2)}) async-start(bf16[8,2,27]{2,1,0:T(2,128)(2,1)} %bitcast.15), calls=%async_computation.2 | async-start | bytes 8192 | tf_op jit(solution)/shard_map/all_to_all | solution.py:121
  35.5 13.6 %all-to-all-start.3 = ((bf16[8,2,128,128]{3,1,2,0:T(2,128)(2,1)}), bf16[8,2,128,128]{3,1,2,0:T(2,128)(2,1)S(1)}, u32[]{:S(2)}, u32[]{:S(2)}) async-start(bf16[8,2,128,128]{3,1,2,0:T(2,128)(2,1)} %copy.66), calls=%async_computation.3 | async-start | bytes 1048576 | tf_op jit(solution)/shard_map/all_to_all | solution.py:119
  49.1 26.2 %all-to-all-start.1 = ((bf16[8,2,128,128]{3,1,2,0:T(2,128)(2,1)}), bf16[8,2,128,128]{3,1,2,0:T(2,128)(2,1)S(1)}, u32[]{:S(2)}, u32[]{:S(2)}) async-start(bf16[8,2,128,128]{3,1,2,0:T(2,128)(2,1)} %copy.62), calls=%async_computation.1 | async-start | bytes 1048576 | tf_op jit(solution)/shard_map/all_to_all | solution.py:120
  53.3 328.6 %all-reduce.6.cloned.1.call-start = ((), (), s32[]{:S(2)}) async-start(), calls=%async_computation.5 | async-start | bytes 4194304 | tf_op jit(solution)/shard_map/psum | solution.py:151
  64.6 8.6 %copy-start.4 = (bf16[11,128,128,1]{2,1,0,3:T(8,128)(2,1)S(1)}, bf16[11,128,128,1]{2,1,0,3:T(8,128)(2,1)}, u32[]{:S(2)}) copy-start(bf16[11,128,128,1]{2,1,0,3:T(8,128)(2,1)} %constant.69) | copy-start | bytes 1081348
  237.9 1.0 copy-start.1
  237.9 1.3 copy-start.2
  239.3 204.9 %all-reduce.4.cloned.1.call-start = ((), (), s32[]{:S(2)}) async-start(), calls=%async_computation.4 | async-start | bytes 131072 | tf_op jit(solution)/shard_map/psum | solution.py:159
Sparse Core Ops, SparseCore 0:
  239.4 142.5 all-reduce.5
  384.8 59.2 all-reduce.3
where the time goes:
time: 456 us; the launch traced here: 452 us
  waiting for transfers between devices  214 us (47%)
  local copies, waits for them, and re-layouts  103 us (23%)
  loops' own time  63 us (14%)
  matrix products  27.9 us (6%)
  starting transfers between devices  23.3 us (5%)
  between operations  14.2 us (3%)
  other arithmetic  6.94 us (2%)
    psum x1, waiting for transfers between devices, on_device(): flux_total, weight_total = lax.psum((flux_sum, weight_sum), 'group')  143 us
    another operation x1, loops' own time, on_device(): flux_sum, weight_sum = lax.fori_loop(0, slot_total, place, (empty, empty))  63 us
    psum x1, waiting for transfers between devices, on_device(): chi_total = lax.psum(chi_local, 'band')  60.6 us
    dynamic_update_slice x16, local copies, waits for them, and re-layouts, place(): flux_sum = lax.dynamic_update_slice(flux_sum, region, corner)  28 us
    dynamic_update_slice x16, local copies, waits for them, and re-layouts, place(): weight_sum = lax.dynamic_update_slice(weight_sum, region, corner)  28 us
    dot_general x2, matrix products, match_block(): jnp.einsum('nyfx,nfg->nygx', rowpass, mixing, precision=lax.Precision.HIG...  17.3 us
    dynamic_slice x32, local copies, waits for them, and re-layouts, place(): weight_got[slot_index]  15 us
    dynamic_slice x32, local copies, waits for them, and re-layouts, place(): weighted[slot_index]  15 us
  transfers between devices with their start and end apart: 6, of which 4 were waited for; matrix products, arithmetic and copies ran while one was open for 7% of the time, Pallas kernels for 0%

commit v1 on v0

v1 whole, which is shorter than its diff:
```python
import functools

import jax
import jax.numpy as jnp
import ml_dtypes
import numpy as np
from jax import lax
from jax.experimental import pallas as pl
from jax.experimental.pallas import tpu as pltpu
from jax.sharding import PartitionSpec as P

PATCH_SIDE = 512
TILE = 128
TILES_DEV = 8
PATCHES = 8
CAP = 2
SPREADS = (0.7, 1.5, 3.0)
DEGREES = (4, 2, 2)
REACH = 10
STARTS = (0, 5, 8)
FILTERS = 11
META_ROWS = 16
STRIP = 32
STRIPS = PATCH_SIDE // STRIP
COL_BLOCKS = PATCH_SIDE // TILE
F32 = jnp.float32
BF16 = jnp.bfloat16


def basis_filters():
    offsets_axis = np.arange(-REACH, REACH + 1) * 1.0
    filters = []
    for spread_value, degree in zip(SPREADS, DEGREES):
        profile = np.exp(-(offsets_axis**2) / (2.0 * spread_value * spread_value))
        profile = profile / profile.sum()
        for exponent in range(degree + 1):
            filters.append(profile * (offsets_axis / REACH) ** exponent)
    return np.stack(filters)


def band_tables():
    filters = basis_filters()
    source = np.arange(TILE)[:, None]
    target = np.arange(TILE)[None, :]
    shift_table = target - source
    inside = np.abs(shift_table) <= REACH
    picked = filters[:, np.clip(shift_table + REACH, 0, 2 * REACH)] * inside
    row_table = np.transpose(picked, (1, 0, 2)).reshape(TILE, FILTERS * TILE)
    column_table = np.transpose(picked, (2, 0, 1)).reshape(TILE, FILTERS * TILE)
    half = lambda table: table.astype(np.float32).astype(ml_dtypes.bfloat16)
    return half(row_table), half(column_table)


def term_list():
    terms = [[] for _ in range(FILTERS)]
    counter = 0
    for family, degree in enumerate(DEGREES):
        for along_x in range(degree + 1):
            for along_y in range(degree + 1 - along_x):
                terms[STARTS[family] + along_y].append((STARTS[family] + along_x, counter))
                counter += 1
    return terms


TERM_LIST = term_list()


def slot_of(owner_ref, tile):
    patch = owner_ref[tile, 0]
    rank = jnp.int32(0)
    for other in range(tile):
        rank = rank + jnp.where(owner_ref[other, 0] == patch, 1, 0).astype(jnp.int32)
    return patch, rank


def masked_weight(var_tile, pads_ref, tile):
    line_y = lax.broadcasted_iota(jnp.int32, (TILE, TILE), 0)
    line_x = lax.broadcasted_iota(jnp.int32, (TILE, TILE), 1)
    inside = (
        (line_y >= pads_ref[tile, 0])
        & (line_y < TILE - pads_ref[tile, 1])
        & (line_x >= pads_ref[tile, 2])
        & (line_x < TILE - pads_ref[tile, 3])
    )
    return jnp.where(inside, var_tile.astype(F32), 0.0)


def weight_kernel(owner_ref, offsets_ref, pads_ref, var_ref, out_ref):
    out_ref[...] = jnp.zeros_like(out_ref)
    line = lax.broadcasted_iota(jnp.int32, (META_ROWS, TILE), 0)
    for tile in range(TILES_DEV):
        patch, rank = slot_of(owner_ref, tile)
        start = pl.multiple_of(rank * TILE, TILE)
        out_ref[patch, pl.ds(start, TILE), :] = masked_weight(
            var_ref[tile], pads_ref, tile
        ).astype(BF16)
        row_offset = offsets_ref[tile, 0].astype(F32)
        col_offset = offsets_ref[tile, 1].astype(F32)
        place = line - rank * 4
        entry = jnp.where(
            place == 0, 1.0, jnp.where(place == 1, row_offset, jnp.where(place == 2, col_offset, 0.0))
        )
        meta = out_ref[patch, CAP * TILE :, :].astype(F32)
        out_ref[patch, CAP * TILE :, :] = (meta + entry).astype(BF16)


def match_kernel(
    owner_ref, pads_ref, coef_ref, flux_ref, var_ref, row_ref, col_ref, out_ref, rowpass, mixed
):
    out_ref[...] = jnp.zeros_like(out_ref)
    for first in range(0, TILES_DEV, 2):
        side = (first // 2) % 2
        pair = flux_ref[first : first + 2].reshape(2 * TILE, TILE)
        rowpass[side] = jnp.dot(pair, row_ref[...], preferred_element_type=F32)
        for part in range(2):
            tile = first + part
            coefs = [coef_ref[tile, k] for k in range(27)]
            for block in range(0, TILE, 16):
                rows = slice(part * TILE + block, part * TILE + block + 16)
                lines = [rowpass[side, rows, f * TILE : (f + 1) * TILE] for f in range(FILTERS)]
                for g in range(FILTERS):
                    total = None
                    for f, k in TERM_LIST[g]:
                        term = lines[f] * coefs[k]
                        total = term if total is None else total + term
                    mixed[side, g * TILE + block : g * TILE + block + 16,
                          part * TILE : (part + 1) * TILE] = total.astype(BF16)
        matched = jnp.dot(col_ref[...], mixed[side], preferred_element_type=F32)
        for part in range(2):
            tile = first + part
            patch, rank = slot_of(owner_ref, tile)
            start = pl.multiple_of(rank * TILE, TILE)
            weight = masked_weight(var_ref[tile], pads_ref, tile)
            out_ref[patch, pl.ds(start, TILE), :] = (
                weight * matched[:, part * TILE : (part + 1) * TILE]
            ).astype(BF16)


def scatter_kernel(meta_ref, tiles_ref, out_ref, image):
    image[...] = jnp.zeros_like(image)
    lane = lax.broadcasted_iota(jnp.int32, (TILE, TILE), 1)
    for source in range(PATCHES):
        for rank in range(CAP):

            @pl.when(meta_ref[source, rank * 4] != 0)
            def _():
                row = pl.multiple_of(meta_ref[source, rank * 4 + 1] * 8, 8)
                column = meta_ref[source, rank * 4 + 2] * 8
                block = column // TILE
                shift = column - block * TILE
                tile = tiles_ref[source, rank * TILE : (rank + 1) * TILE, :].astype(F32)
                turned = pltpu.roll(tile, shift, 1)
                image[block, pl.ds(row, TILE), :] += jnp.where(lane >= shift, turned, 0.0)
                image[block + 1, pl.ds(row, TILE), :] += jnp.where(lane < shift, turned, 0.0)

    for strip in range(STRIPS):
        for block in range(COL_BLOCKS):
            out_ref[strip, :, block * TILE : (block + 1) * TILE] = image[
                block, strip * STRIP : (strip + 1) * STRIP, :
            ].astype(BF16)


def reduce_kernel(flux_ref, weight_ref, coadd_ref, chi_ref):
    flux = flux_ref[0].astype(F32)
    weight = weight_ref[0].astype(F32)
    for strip in range(1, STRIPS):
        flux = flux + flux_ref[strip].astype(F32)
        weight = weight + weight_ref[strip].astype(F32)
    coadd = flux / (weight + 1.0)
    coadd_ref[...] = coadd
    chi = (flux * coadd).astype(BF16)
    for band in range(chi_ref.shape[0]):
        chi_ref[band] = chi


def chi_kernel(parts_ref, out_ref):
    total = parts_ref[0].astype(F32)
    for band in range(1, parts_ref.shape[0]):
        total = total + parts_ref[band].astype(F32)
    out_ref[...] = total


SMEM = pl.BlockSpec(memory_space=pltpu.SMEM)
VMEM = pl.BlockSpec(memory_space=pltpu.VMEM)
PARAMS = pltpu.CompilerParams(vmem_limit_bytes=32 * 1024 * 1024)


def scatter(meta, tiles):
    return pl.pallas_call(
        scatter_kernel,
        out_shape=jax.ShapeDtypeStruct((STRIPS, STRIP, PATCH_SIDE), BF16),
        in_specs=[SMEM, VMEM],
        out_specs=VMEM,
        scratch_shapes=[pltpu.VMEM((COL_BLOCKS + 1, PATCH_SIDE, TILE), F32)],
        compiler_params=PARAMS,
        cost_estimate=pl.CostEstimate(flops=10_000_000, bytes_accessed=2_000_000, transcendentals=0),
    )(meta, tiles)


def on_device(tile_flux, inverse_var, kernel_coef, owner_index, offsets, pad_widths):
    row_table, column_table = band_tables()
    owner, corner, pads = owner_index[0], offsets[0], pad_widths[0]
    bands = lax.axis_size("band")
    with jax.named_scope("weight_slots"):
        weight_slots = pl.pallas_call(
            weight_kernel,
            out_shape=jax.ShapeDtypeStruct((PATCHES, CAP * TILE + META_ROWS, TILE), BF16),
            in_specs=[SMEM, SMEM, SMEM, VMEM],
            out_specs=VMEM,
            compiler_params=PARAMS,
        )(owner, corner, pads, inverse_var[0])
    weight_got = lax.all_to_all(weight_slots, "patch", 0, 0, tiled=True)
    with jax.named_scope("flux_slots"):
        flux_slots = pl.pallas_call(
            match_kernel,
            out_shape=jax.ShapeDtypeStruct((PATCHES, CAP * TILE, TILE), BF16),
            in_specs=[SMEM, SMEM, SMEM, VMEM, VMEM, VMEM, VMEM],
            out_specs=VMEM,
            scratch_shapes=[
                pltpu.VMEM((2, 2 * TILE, FILTERS * TILE), F32),
                pltpu.VMEM((2, FILTERS * TILE, 2 * TILE), BF16),
            ],
            compiler_params=PARAMS,
            cost_estimate=pl.CostEstimate(
                flops=750_000_000, bytes_accessed=2_000_000, transcendentals=0
            ),
        )(
            owner,
            pads,
            kernel_coef[0].astype(F32),
            tile_flux[0],
            inverse_var[0],
            jnp.asarray(row_table),
            jnp.asarray(column_table),
        )
    flux_got = lax.all_to_all(flux_slots, "patch", 0, 0, tiled=True)
    meta = weight_got[:, CAP * TILE : CAP * TILE + 8, 0].astype(jnp.int32)
    with jax.named_scope("weight_image"):
        weight_image = scatter(meta, weight_got)
    weight_strips = lax.all_to_all(weight_image, "group", 0, 0, tiled=True)
    with jax.named_scope("flux_image"):
        flux_image = scatter(meta, flux_got)
    flux_strips = lax.all_to_all(flux_image, "group", 0, 0, tiled=True)
    with jax.named_scope("strip_sums"):
        coadd, chi_copies = pl.pallas_call(
            reduce_kernel,
            out_shape=(
                jax.ShapeDtypeStruct((STRIP, PATCH_SIDE), F32),
                jax.ShapeDtypeStruct((bands, STRIP, PATCH_SIDE), BF16),
            ),
            in_specs=[VMEM, VMEM],
            out_specs=(VMEM, VMEM),
            compiler_params=PARAMS,
        )(flux_strips, weight_strips)
    chi_parts = lax.all_to_all(chi_copies, "band", 0, 0, tiled=True)
    with jax.named_scope("chi_sum"):
        chi = pl.pallas_call(
            chi_kernel,
            out_shape=jax.ShapeDtypeStruct((STRIP, PATCH_SIDE), F32),
            in_specs=[VMEM],
            out_specs=VMEM,
            compiler_params=PARAMS,
        )(chi_parts)
    return (coadd[None, None], chi[None])


def solution(mesh):
    return jax.shard_map(
        on_device,
        mesh=mesh,
        in_specs=(
            P("band", ("group", "patch"), None, None),
            P("band", ("group", "patch"), None, None),
            P("band", ("group", "patch"), None),
            P("band", ("group", "patch"), None),
            P("band", ("group", "patch"), None),
            P("band", ("group", "patch"), None),
        ),
        out_specs=(P("band", "patch", "group", None), P("patch", "group", None)),
        check_vma=False,
    )
```

time: 456 us -> 125 us (0.27)
  the two profiles are of different devices: /device:TPU:1 before, /device:TPU:2 now
where the time goes in v1:
time: 125 us; the launch traced here: 124 us
  blocking collectives  43.9 us (35%)
  waiting for transfers between devices  42.4 us (34%)
  starting transfers between devices  23.3 us (19%)
  Pallas kernels  10.4 us (8%)
  local copies, waits for them, and re-layouts  3.14 us (3%)
    all_to_all x1, blocking collectives, on_device(): flux_strips = lax.all_to_all(flux_image, 'group', 0, 0, tiled=True)  34.7 us
    all_to_all x1, waiting for transfers between devices, on_device(): weight_strips = lax.all_to_all(weight_image, 'group', 0, 0, tiled=True)  27.4 us
    all_to_all x1, starting transfers between devices, on_device(): weight_strips = lax.all_to_all(weight_image, 'group', 0, 0, tiled=True)  15.2 us
    all_to_all x1, blocking collectives, on_device(): chi_parts = lax.all_to_all(chi_copies, 'band', 0, 0, tiled=True)  9.13 us
    all_to_all x1, waiting for transfers between devices, on_device(): flux_got = lax.all_to_all(flux_slots, 'patch', 0, 0, tiled=True)  7.79 us
    all_to_all x1, waiting for transfers between devices, on_device(): weight_got = lax.all_to_all(weight_slots, 'patch', 0, 0, tiled=True)  7.18 us
    all_to_all x1, starting transfers between devices, on_device(): weight_got = lax.all_to_all(weight_slots, 'patch', 0, 0, tiled=True)  4.61 us
    pallas_call x2, Pallas kernels, scatter(): pl.pallas_call(scatter_kernel, out_shape=jax.ShapeDtypeStruct((STRIPS, ST...  3.72 us
  transfers between devices with their start and end apart: 3, of which 3 were waited for; matrix products, arithmetic and copies ran while one was open for 0% of the time, Pallas kernels for 6%

profile of v1, /device:TPU:2, one launch (start us, length us, event | category | flops | bytes accessed | tf_op | source)
XLA Modules:
  0.0 124.0 jit_solution(12625666033513739919)
XLA Ops:
  0.6 0.0 copy-start.8
  0.6 0.6 copy-done.8
  1.3 0.0 copy-start.5
  1.3 0.1 copy.15.owner_ref
  1.4 0.6 copy-done.5
  2.0 0.1 copy.17.pads_ref
  2.0 0.0 copy-start.7
  2.1 0.7 copy-done.7
  2.7 0.1 copy.16.offsets_ref
  2.8 0.0 copy-start
  2.8 0.9 copy-done
  3.8 0.0 copy-start.4
  3.8 1.8 %weight_slots.1 = bf16[8,272,128]{2,1,0:T(8,128)(2,1)} custom-call(s32[8,1]{1,0:T(8,128)S(1)} %copy.15.owner_ref, s32[8,2]{1,0:T(8,128)S(1)} %copy.16.offsets_ref, s32[8,4]{1,0:T(8,128)S(1)} %copy.17.pads_ref, bf16[8,128,128]{2,1,0:T(8,128)(2,1)S(1)} %bitcast.10), custom_call_target="tpu_custom_call" | custom-call | tf_op jit(solution)/shard_map/weight_slots/pallas_call | solution.py:205
  5.6 4.6 %all-to-all-start = ((bf16[8,272,128]{2,1,0:T(8,128)(2,1)}), bf16[8,272,128]{2,1,0:T(8,128)(2,1)S(1)}, u32[]{:S(2)}, u32[]{:S(2)}) async-start(bf16[8,272,128]{2,1,0:T(8,128)(2,1)} %weight_slots.1), calls=%async_computation | async-start | bytes 1114112 | tf_op jit(solution)/shard_map/all_to_all | solution.py:212
  10.2 0.0 copy-done.6
  10.2 0.0 copy-done.4
  10.2 0.0 copy-done.1
  10.2 0.0 copy-done.2
  10.2 0.0 copy-done.3
  10.2 3.5 %flux_slots.1 = bf16[8,256,128]{2,1,0:T(8,128)(2,1)} custom-call(s32[8,1]{1,0:T(8,128)S(1)} %copy.15.owner_ref, s32[8,4]{1,0:T(8,128)S(1)} %copy.17.pads_ref, f32[8,27]{1,0:T(8,128)S(1)} %bitcast_convert_fusion.coef_ref, bf16[8,128,128]{2,1,0:T(8,128)(2,1)S(1)} %bitcast.12, bf16[8,128,128]{2,1,0:T(8,128)(2,1)S(1)} %bitcast.11, ...), custom_call_target="tpu_custom_call" | custom-call | flops 750000000 | bytes 2000000 | tf_op jit(solution)/shard_map/flux_slots/pallas_call | solution.py:214
  13.7 7.2 %all-to-all-done.tiles_ref = bf16[8,272,128]{2,1,0:T(8,128)(2,1)S(1)} async-done(((bf16[8,272,128]{2,1,0:T(8,128)(2,1)}), bf16[8,272,128]{2,1,0:T(8,128)(2,1)S(1)}, u32[]{:S(2)}, u32[]{:S(2)}) %all-to-all-start) | async-done | bytes 557088 | tf_op jit(solution)/shard_map/all_to_all | solution.py:212
  20.9 3.5 %all-to-all-start.1 = ((bf16[8,256,128]{2,1,0:T(8,128)(2,1)}), bf16[8,256,128]{2,1,0:T(8,128)(2,1)S(1)}, u32[]{:S(2)}, u32[]{:S(2)}) async-start(bf16[8,256,128]{2,1,0:T(8,128)(2,1)} %flux_slots.1), calls=%async_computation.1 | async-start | bytes 1048576 | tf_op jit(solution)/shard_map/all_to_all | solution.py:236
  24.4 0.2 convert_reduce_fusion.meta_ref
  24.6 2.3 %weight_image.1 = bf16[16,32,512]{2,1,0:T(8,128)(2,1)} custom-call(s32[8,8]{1,0:T(8,128)S(1)} %convert_reduce_fusion.meta_ref, bf16[8,272,128]{2,1,0:T(8,128)(2,1)S(1)} %all-to-all-done.tiles_ref), custom_call_target="tpu_custom_call" | custom-call | flops 10000000 | bytes 2000000 | tf_op jit(solution)/shard_map/weight_image/pallas_call | solution.py:189
  26.9 7.8 %all-to-all-done.1.tiles_ref = bf16[8,256,128]{2,1,0:T(8,128)(2,1)S(1)} async-done(((bf16[8,256,128]{2,1,0:T(8,128)(2,1)}), bf16[8,256,128]{2,1,0:T(8,128)(2,1)S(1)}, u32[]{:S(2)}, u32[]{:S(2)}) %all-to-all-start.1) | async-done | bytes 524320 | tf_op jit(solution)/shard_map/all_to_all | solution.py:236
  34.7 15.2 %all-to-all-start.3 = ((bf16[16,32,512]{2,1,0:T(8,128)(2,1)}), bf16[16,32,512]{2,1,0:T(8,128)(2,1)S(1)}, u32[]{:S(2)}, u32[]{:S(2)}) async-start(bf16[16,32,512]{2,1,0:T(8,128)(2,1)} %weight_image.1), calls=%async_computation.3 | async-start | bytes 1048576 | tf_op jit(solution)/shard_map/all_to_all | solution.py:240
  49.9 1.5 %flux_image.1 = bf16[16,32,512]{2,1,0:T(8,128)(2,1)S(1)} custom-call(s32[8,8]{1,0:T(8,128)S(1)} %convert_reduce_fusion.meta_ref, bf16[8,256,128]{2,1,0:T(8,128)(2,1)S(1)} %all-to-all-done.1.tiles_ref), custom_call_target="tpu_custom_call" | custom-call | flops 10000000 | bytes 2000000 | tf_op jit(solution)/shard_map/flux_image/pallas_call | solution.py:189
  51.3 27.4 %all-to-all-done.3.weight_ref = bf16[16,32,512]{2,1,0:T(8,128)(2,1)S(1)} async-done(((bf16[16,32,512]{2,1,0:T(8,128)(2,1)}), bf16[16,32,512]{2,1,0:T(8,128)(2,1)S(1)}, u32[]{:S(2)}, u32[]{:S(2)}) %all-to-all-start.3) | async-done | bytes 524320 | tf_op jit(solution)/shard_map/all_to_all | solution.py:240
  78.7 34.7 %all_to_all.25.flux_ref = bf16[16,32,512]{2,1,0:T(8,128)(2,1)S(1)} all-to-all(bf16[16,32,512]{2,1,0:T(8,128)(2,1)S(1)} %flux_image.1), channel_id=1, replica_groups=mesh['band'=4,'group'=16,'patch'=8] {'group'}, dimensions={0} | all-to-all | bytes 1048576 | tf_op jit(solution)/shard_map/all_to_all | solution.py:243
  113.5 0.8 strip_sums.1
  114.2 9.1 %all_to_all.26.parts_ref = bf16[4,32,512]{2,1,0:T(8,128)(2,1)S(1)} all-to-all(bf16[4,32,512]{2,1,0:T(8,128)(2,1)S(1)} %get-tuple-element.5), channel_id=1, replica_groups=mesh['band'=4,'group'=16,'patch'=8] {'band'}, dimensions={0} | all-to-all | bytes 262144 | tf_op jit(solution)/shard_map/all_to_all | solution.py:255
  123.4 0.6 chi_sum.1
  (5 shorter events, 0.0 us)
Async XLA Ops:
  0.6 0.7 copy-start.8
  1.3 0.7 copy-start.5
  2.0 0.7 copy-start.7
  2.8 0.9 copy-start
  3.8 6.4 %copy-start.4 = (bf16[128,1408]{1,0:T(8,128)(2,1)S(1)}, bf16[128,1408]{1,0:T(8,128)(2,1)}, u32[]{:S(2)}) copy-start(bf16[128,1408]{1,0:T(8,128)(2,1)} %constant.5.clone.col_ref) | copy-start | bytes 1081348
  5.6 4.6 %copy-start.6 = (bf16[1,8,27]{2,1,0:T(8,128)(2,1)S(1)}, bf16[1,8,27]{2,1,0:T(8,128)(2,1)}, u32[]{:S(2)}) copy-start(bf16[1,8,27]{2,1,0:T(8,128)(2,1)} %param.10) | copy-start | bytes 1300
  5.6 4.7 %copy-start.1 = (bf16[1,8,128,128]{3,2,1,0:T(8,128)(2,1)S(1)}, bf16[1,8,128,128]{3,2,1,0:T(8,128)(2,1)}, u32[]{:S(2)}) copy-start(bf16[1,8,128,128]{3,2,1,0:T(8,128)(2,1)} %param.9) | copy-start | bytes 786436
  5.6 4.7 %copy-start.2 = (bf16[1,8,128,128]{3,2,1,0:T(8,128)(2,1)S(1)}, bf16[1,8,128,128]{3,2,1,0:T(8,128)(2,1)}, u32[]{:S(2)}) copy-start(bf16[1,8,128,128]{3,2,1,0:T(8,128)(2,1)} %param.8) | copy-start | bytes 786436
  5.6 4.7 %copy-start.3 = (bf16[128,1408]{1,0:T(8,128)(2,1)S(1)}, bf16[128,1408]{1,0:T(8,128)(2,1)}, u32[]{:S(2)}) copy-start(bf16[128,1408]{1,0:T(8,128)(2,1)} %constant.4.clone.row_ref) | copy-start | bytes 1081348
  5.6 15.3 %all-to-all-start = ((bf16[8,272,128]{2,1,0:T(8,128)(2,1)}), bf16[8,272,128]{2,1,0:T(8,128)(2,1)S(1)}, u32[]{:S(2)}, u32[]{:S(2)}) async-start(bf16[8,272,128]{2,1,0:T(8,128)(2,1)} %weight_slots.1), calls=%async_computation | async-start | bytes 1114112 | tf_op jit(solution)/shard_map/all_to_all | solution.py:212
  20.9 13.8 %all-to-all-start.1 = ((bf16[8,256,128]{2,1,0:T(8,128)(2,1)}), bf16[8,256,128]{2,1,0:T(8,128)(2,1)S(1)}, u32[]{:S(2)}, u32[]{:S(2)}) async-start(bf16[8,256,128]{2,1,0:T(8,128)(2,1)} %flux_slots.1), calls=%async_computation.1 | async-start | bytes 1048576 | tf_op jit(solution)/shard_map/all_to_all | solution.py:236
  34.7 44.1 %all-to-all-start.3 = ((bf16[16,32,512]{2,1,0:T(8,128)(2,1)}), bf16[16,32,512]{2,1,0:T(8,128)(2,1)S(1)}, u32[]{:S(2)}, u32[]{:S(2)}) async-start(bf16[16,32,512]{2,1,0:T(8,128)(2,1)} %weight_image.1), calls=%async_computation.3 | async-start | bytes 1048576 | tf_op jit(solution)/shard_map/all_to_all | solution.py:240

commit v2 on v1

v2 whole, which is shorter than its diff:
```python
import jax
import jax.numpy as jnp
import ml_dtypes
import numpy as np
from jax import lax
from jax.experimental import pallas as pl
from jax.experimental.pallas import tpu as pltpu
from jax.sharding import PartitionSpec as P

PATCH_SIDE = 512
TILE = 128
TILES_DEV = 8
PATCHES = 8
CAP = 2
SPREADS = (0.7, 1.5, 3.0)
DEGREES = (4, 2, 2)
REACH = 10
STARTS = (0, 5, 8)
FILTERS = 11
META_ROWS = 16
SLOT_ROWS = 2 * CAP * 64
STRIP = 32
STRIPS = PATCH_SIDE // STRIP
HALF = STRIPS // 2
COL_BLOCKS = PATCH_SIDE // TILE
F32 = jnp.float32
BF16 = jnp.bfloat16


def basis_filters():
    offsets_axis = np.arange(-REACH, REACH + 1) * 1.0
    filters = []
    for spread_value, degree in zip(SPREADS, DEGREES):
        profile = np.exp(-(offsets_axis**2) / (2.0 * spread_value * spread_value))
        profile = profile / profile.sum()
        for exponent in range(degree + 1):
            filters.append(profile * (offsets_axis / REACH) ** exponent)
    return np.stack(filters)


def band_tables():
    filters = basis_filters()
    source = np.arange(TILE)[:, None]
    target = np.arange(TILE)[None, :]
    shift_table = target - source
    inside = np.abs(shift_table) <= REACH
    picked = filters[:, np.clip(shift_table + REACH, 0, 2 * REACH)] * inside
    row_table = np.transpose(picked, (1, 0, 2)).reshape(TILE, FILTERS * TILE)
    column_table = np.transpose(picked, (2, 0, 1)).reshape(TILE, FILTERS * TILE)
    half = lambda table: table.astype(np.float32).astype(ml_dtypes.bfloat16)
    return half(row_table), half(column_table)


def term_list():
    terms = [[] for _ in range(FILTERS)]
    counter = 0
    for family, degree in enumerate(DEGREES):
        for along_x in range(degree + 1):
            for along_y in range(degree + 1 - along_x):
                terms[STARTS[family] + along_y].append((STARTS[family] + along_x, counter))
                counter += 1
    return terms


TERM_LIST = term_list()


def slot_of(owner_ref, offsets_ref, tile):
    patch = owner_ref[0, tile]
    rank = jnp.int32(0)
    before = [jnp.int32(0), jnp.int32(0)]
    for other in range(tile):
        same = owner_ref[0, other] == patch
        rank = rank + jnp.where(same, 1, 0)
        before = [v + jnp.where(same, offsets_ref[i, other], 0) for i, v in enumerate(before)]
    return patch, rank, before


def first_row(row_offset, parity):
    row = row_offset * 8
    return (row // 64) * STRIP + jnp.clip(row % 64 - STRIP * parity, 0, STRIP)


def masked_weight(var_tile, pads_ref, tile):
    line_y = lax.broadcasted_iota(jnp.int32, (TILE, TILE), 0)
    line_x = lax.broadcasted_iota(jnp.int32, (TILE, TILE), 1)
    inside = (
        (line_y >= pads_ref[0, tile])
        & (line_y < TILE - pads_ref[1, tile])
        & (line_x >= pads_ref[2, tile])
        & (line_x < TILE - pads_ref[3, tile])
    )
    return jnp.where(inside, var_tile.astype(F32), 0.0)


def slot_kernel(
    owner_ref, offsets_ref, pads_ref, coef_hbm, flux_hbm, var_hbm, row_hbm, col_hbm, out_ref,
    coef_half, coef_full, coef_ref, flux_ref, var_ref, row_ref, col_ref, rowpass, mixed, whole, sems,
):
    pairs = (
        (coef_hbm, coef_half),
        (row_hbm, row_ref),
        (flux_hbm, flux_ref),
        (col_hbm, col_ref),
        (var_hbm, var_ref),
    )
    copies = [pltpu.make_async_copy(a, b, sems.at[i]) for i, (a, b) in enumerate(pairs)]
    for copy in copies:
        copy.start()
    out_ref[...] = jnp.zeros_like(out_ref)
    line = lax.broadcasted_iota(jnp.int32, (META_ROWS, TILE), 0)
    slots = []
    for tile in range(TILES_DEV):
        patch, rank, before = slot_of(owner_ref, offsets_ref, tile)
        slots.append((patch, rank))
        now = [offsets_ref[0, tile], offsets_ref[1, tile]]
        second = rank > 0
        entry = [jnp.int32(1)] + [jnp.where(second, u, v) for u, v in zip(before, now)]
        entry = entry + [jnp.int32(0), rank] + [jnp.where(second, v, 0) for v in now]
        meta = jnp.zeros((META_ROWS, TILE), F32)
        for i, value in enumerate(entry):
            if i != 3:
                meta = jnp.where(line == i, value.astype(F32), meta)
        meta = meta.astype(BF16)
        for parity in range(2):
            out_ref[parity * PATCHES + patch, SLOT_ROWS:, :] = meta
    copies[0].wait()
    coef_full[...] = coef_half[...].astype(F32)
    spread = pltpu.make_async_copy(coef_full, coef_ref, sems.at[5])
    spread.start()
    copies[1].wait()
    copies[2].wait()
    for first in range(0, TILES_DEV, 2):
        side = (first // 2) % 2
        pair = flux_ref[first : first + 2].reshape(2 * TILE, TILE)
        rowpass[side] = jnp.dot(pair, row_ref[...], preferred_element_type=F32)
        for part in range(2):
            if first + part == 0:
                spread.wait()
            coefs = [coef_ref[first + part, k] for k in range(27)]
            for block in range(0, TILE, 16):
                rows = slice(part * TILE + block, part * TILE + block + 16)
                lines = [rowpass[side, rows, f * TILE : (f + 1) * TILE] for f in range(FILTERS)]
                for g in range(FILTERS):
                    total = None
                    for f, k in TERM_LIST[g]:
                        term = lines[f] * coefs[k]
                        total = term if total is None else total + term
                    mixed[side, g * TILE + block : g * TILE + block + 16,
                          part * TILE : (part + 1) * TILE] = total.astype(BF16)
        if first == 0:
            copies[3].wait()
            copies[4].wait()
        matched = jnp.dot(col_ref[...], mixed[side], preferred_element_type=F32)
        for part in range(2):
            tile = first + part
            patch, rank = slots[tile]
            weight = masked_weight(var_ref[tile], pads_ref, tile)
            whole[side, part, 0] = weight * matched[:, part * TILE : (part + 1) * TILE]
            whole[side, part, 1] = weight
            for parity in range(2):
                top = first_row(offsets_ref[0, tile], parity)
                taken = []
                for group in range(8):
                    at = top + 8 * group
                    row = (at // STRIP) * 64 + STRIP * parity + at % STRIP - offsets_ref[0, tile] * 8
                    taken.append(pl.multiple_of(row, 8))
                for image in range(2):
                    start = pl.multiple_of(image * CAP * 64 + rank * 64, 64)
                    rows = [whole[side, part, image, pl.ds(row, 8), :] for row in taken]
                    out_ref[parity * PATCHES + patch, pl.ds(start, 64), :] = jnp.concatenate(
                        rows, axis=0
                    ).astype(BF16)


def scatter_kernel(meta_ref, slots_ref, out_ref, images):
    images[...] = jnp.zeros_like(images)
    parity = lax.rem(lax.axis_index("group"), 2)
    lane = lax.broadcasted_iota(jnp.int32, (64, TILE), 1)
    for source in range(2 * PATCHES):
        for rank in range(CAP):

            @pl.when(meta_ref[source, rank * 4] != 0)
            def _():
                row = pl.multiple_of(first_row(meta_ref[source, rank * 4 + 1], parity), 8)
                column = meta_ref[source, rank * 4 + 2] * 8
                block = column // TILE
                shift = column % TILE
                for image in range(2):
                    start = image * CAP * 64 + rank * 64
                    half = slots_ref[source, start : start + 64, :].astype(F32)
                    turned = pltpu.roll(half, shift, 1)
                    place = (image, block, pl.ds(row, 64), slice(None))
                    images[place] += jnp.where(lane >= shift, turned, 0.0)
                    place = (image, block + 1, pl.ds(row, 64), slice(None))
                    images[place] += jnp.where(lane < shift, turned, 0.0)

    for half in range(HALF):
        for image in range(2):
            for block in range(COL_BLOCKS):
                out_ref[half, image, :, block * TILE : (block + 1) * TILE] = images[
                    image, block, half * STRIP : (half + 1) * STRIP, :
                ].astype(BF16)


def reduce_kernel(strips_ref, coadd_ref, chi_ref):
    flux = strips_ref[0, 0].astype(F32)
    weight = strips_ref[0, 1].astype(F32)
    for half in range(1, HALF):
        flux = flux + strips_ref[half, 0].astype(F32)
        weight = weight + strips_ref[half, 1].astype(F32)
    coadd = flux / (weight + 1.0)
    coadd_ref[...] = coadd
    chi = (flux * coadd).astype(BF16)
    for band in range(chi_ref.shape[0]):
        chi_ref[band] = chi


def chi_kernel(parts_ref, out_ref):
    total = parts_ref[0].astype(F32)
    for band in range(1, parts_ref.shape[0]):
        total = total + parts_ref[band].astype(F32)
    out_ref[...] = total


SMEM = pl.BlockSpec(memory_space=pltpu.SMEM)
VMEM = pl.BlockSpec(memory_space=pltpu.VMEM)
HBM = pl.BlockSpec(memory_space=pltpu.HBM)
VMEM_ALL = 60 * 1024 * 1024
PARAMS = pltpu.CompilerParams(vmem_limit_bytes=32 * 1024 * 1024)


def on_device(tile_flux, inverse_var, kernel_coef, owner_index, offsets, pad_widths):
    row_table, column_table = band_tables()
    owner, corner, pads = owner_index[0].T, offsets[0].T, pad_widths[0].T
    bands = lax.axis_size("band")
    with jax.named_scope("tile_slots"):
        slots = pl.pallas_call(
            slot_kernel,
            out_shape=jax.ShapeDtypeStruct((2 * PATCHES, SLOT_ROWS + META_ROWS, TILE), BF16),
            in_specs=[SMEM] * 3 + [HBM] * 5,
            out_specs=VMEM,
            scratch_shapes=[
                pltpu.VMEM((TILES_DEV, 27), BF16),
                pltpu.VMEM((TILES_DEV, 27), F32),
                pltpu.SMEM((TILES_DEV, 27), F32),
                pltpu.VMEM((TILES_DEV, TILE, TILE), BF16),
                pltpu.VMEM((TILES_DEV, TILE, TILE), BF16),
                pltpu.VMEM((TILE, FILTERS * TILE), BF16),
                pltpu.VMEM((TILE, FILTERS * TILE), BF16),
                pltpu.VMEM((2, 2 * TILE, FILTERS * TILE), F32),
                pltpu.VMEM((2, FILTERS * TILE, 2 * TILE), BF16),
                pltpu.VMEM((2, 2, 2, TILE, TILE), F32),
                pltpu.SemaphoreType.DMA((6,)),
            ],
            compiler_params=pltpu.CompilerParams(vmem_limit_bytes=VMEM_ALL),
        )(
            owner,
            corner,
            pads,
            kernel_coef[0],
            tile_flux[0],
            inverse_var[0],
            jnp.asarray(row_table),
            jnp.asarray(column_table),
        )
    blocks = [
        [z * PATCHES + patch for z in (low, low + 1) for patch in range(PATCHES)]
        for low in range(0, STRIPS, 2)
    ]
    slots_got = lax.all_to_all(
        slots, ("group", "patch"), 0, 0, tiled=True, axis_index_groups=blocks
    )
    meta = slots_got[:, SLOT_ROWS : SLOT_ROWS + 8, 0].astype(jnp.int32)
    with jax.named_scope("strip_images"):
        strips = pl.pallas_call(
            scatter_kernel,
            out_shape=jax.ShapeDtypeStruct((HALF, 2, STRIP, PATCH_SIDE), BF16),
            in_specs=[SMEM, VMEM],
            out_specs=VMEM,
            scratch_shapes=[pltpu.VMEM((2, COL_BLOCKS + 1, PATCH_SIDE // 2, TILE), F32)],
            compiler_params=PARAMS,
        )(meta, slots_got)
    parities = [list(range(parity, STRIPS, 2)) for parity in range(2)]
    strips_got = lax.all_to_all(strips, "group", 0, 0, tiled=True, axis_index_groups=parities)
    with jax.named_scope("strip_sums"):
        coadd, chi_copies = pl.pallas_call(
            reduce_kernel,
            out_shape=(
                jax.ShapeDtypeStruct((STRIP, PATCH_SIDE), F32),
                jax.ShapeDtypeStruct((bands, STRIP, PATCH_SIDE), BF16),
            ),
            in_specs=[VMEM],
            out_specs=(VMEM, VMEM),
            compiler_params=PARAMS,
        )(strips_got)
    chi_parts = lax.all_to_all(chi_copies, "band", 0, 0, tiled=True)
    with jax.named_scope("chi_sum"):
        chi = pl.pallas_call(
            chi_kernel,
            out_shape=jax.ShapeDtypeStruct((STRIP, PATCH_SIDE), F32),
            in_specs=[VMEM],
            out_specs=VMEM,
            compiler_params=PARAMS,
        )(chi_parts)
    return (coadd[None, None], chi[None])


def solution(mesh):
    return jax.shard_map(
        on_device,
        mesh=mesh,
        in_specs=(
            P("band", ("group", "patch"), None, None),
            P("band", ("group", "patch"), None, None),
            P("band", ("group", "patch"), None),
            P("band", ("group", "patch"), None),
            P("band", ("group", "patch"), None),
            P("band", ("group", "patch"), None),
        ),
        out_specs=(P("band", "patch", "group", None), P("patch", "group", None)),
        check_vma=False,
    )
```

time: 125 us -> 88.8 us (0.71)
  the two profiles are of different devices: /device:TPU:2 before, /device:TPU:1 now
where the time goes in v2:
time: 88.8 us; the launch traced here: 88.4 us
  blocking collectives  78.6 us (89%)
  Pallas kernels  9.03 us (10%)
    all_to_all x1, blocking collectives, on_device(): lax.all_to_all(strips, 'group', 0, 0, tiled=True, axis_index_groups=parit...  38.4 us
    all_to_all x1, blocking collectives, on_device(): lax.all_to_all(slots, ('group', 'patch'), 0, 0, tiled=True, axis_index_gr...  27.3 us
    all_to_all x1, blocking collectives, on_device(): chi_parts = lax.all_to_all(chi_copies, 'band', 0, 0, tiled=True)  12.9 us
    pallas_call x1, Pallas kernels, on_device(): pl.pallas_call(slot_kernel, out_shape=jax.ShapeDtypeStruct((2 * PATCHES,...  5.54 us
    pallas_call x1, Pallas kernels, on_device(): pl.pallas_call(scatter_kernel, out_shape=jax.ShapeDtypeStruct((HALF, 2, S...  2.13 us

profile of v2, /device:TPU:1, one launch (start us, length us, event | category | flops | bytes accessed | tf_op | source)
XLA Modules:
  0.0 88.4 jit_solution(2918417489842116249)
XLA Ops:
  0.6 5.5 %tile_slots.1 = bf16[16,272,128]{2,1,0:T(8,128)(2,1)} custom-call(s32[1,8]{1,0:T(1,128)} %bitcast.21, s32[2,8]{1,0:T(2,128)} %bitcast.20, s32[4,8]{1,0:T(4,128)} %bitcast.18, bf16[8,27]{1,0:T(8,128)(2,1)} %bitcast.19, bf16[8,128,128]{2,1,0:T(8,128)(2,1)} %bitcast.15, bf16[8,128,128]{2,1,0:T(8,128)(2,1)} %bitcast.16, ...), custom_call_target="tpu_custom_call" | custom-call | tf_op jit(solution)/shard_map/tile_slots/pallas_call | solution.py:238
  6.2 27.3 %all_to_all.15.slots_ref = bf16[16,272,128]{2,1,0:T(8,128)(2,1)S(1)} all-to-all(bf16[16,272,128]{2,1,0:T(8,128)(2,1)} %tile_slots.1), channel_id=1, replica_groups={{0,1,2,3,4,5,6,7,8,9,10,11,12,13,14,15},{16,17,18,19,20,21,22,23,24,25,..., dimensions={0} | all-to-all | bytes 2228224 | tf_op jit(solution)/shard_map/all_to_all | solution.py:271
  33.5 0.2 copy.14
  33.6 2.1 %strip_images.1 = bf16[8,2,32,512]{3,2,1,0:T(8,128)(2,1)S(1)} custom-call(s32[16,8]{1,0:T(8,128)S(1)} %bitcast.14, bf16[16,272,128]{2,1,0:T(8,128)(2,1)S(1)} %all_to_all.15.slots_ref), custom_call_target="tpu_custom_call" | custom-call | tf_op jit(solution)/shard_map/strip_images/pallas_call | solution.py:276
  35.8 38.4 %all_to_all.16.strips_ref = bf16[8,2,32,512]{3,2,1,0:T(8,128)(2,1)S(1)} all-to-all(bf16[8,2,32,512]{3,2,1,0:T(8,128)(2,1)S(1)} %strip_images.1), channel_id=1, replica_groups={{0,16,32,48,64,80,96,112},{8,24,40,56,72,88,104,120},{1,17,33,49,65,81,..., dimensions={0} | all-to-all | bytes 1048576 | tf_op jit(solution)/shard_map/all_to_all | solution.py:285
  74.2 0.7 strip_sums.1
  74.9 12.9 %all_to_all.17.parts_ref = bf16[4,32,512]{2,1,0:T(8,128)(2,1)S(1)} all-to-all(bf16[4,32,512]{2,1,0:T(8,128)(2,1)S(1)} %get-tuple-element.5), channel_id=1, replica_groups=mesh['band'=4,'group'=16,'patch'=8] {'band'}, dimensions={0} | all-to-all | bytes 262144 | tf_op jit(solution)/shard_map/all_to_all | solution.py:297
  87.8 0.6 chi_sum.1
  (1 shorter events, 0.0 us)

commit v3 on v2

--- a/solution.py
+++ b/solution.py
@@ -94,21 +94,30 @@
 
 
 def slot_kernel(
-    owner_ref, offsets_ref, pads_ref, coef_hbm, flux_hbm, var_hbm, row_hbm, col_hbm, out_ref,
-    coef_half, coef_full, coef_ref, flux_ref, var_ref, row_ref, col_ref, rowpass, mixed, whole, sems,
+    owner_hbm, offsets_hbm, pads_hbm, coef_hbm, flux_hbm, var_hbm, row_hbm, col_hbm, out_hbm,
+    owner_ref, offsets_ref, pads_ref, coef_half, coef_full, coef_ref, flux_ref, var_ref, row_ref,
+    col_ref, rowpass, mixed, whole, halves, metas, sems, out_sems,
 ):
     pairs = (
+        (owner_hbm, owner_ref),
+        (offsets_hbm, offsets_ref),
         (coef_hbm, coef_half),
         (row_hbm, row_ref),
         (flux_hbm, flux_ref),
+        (pads_hbm, pads_ref),
         (col_hbm, col_ref),
         (var_hbm, var_ref),
     )
     copies = [pltpu.make_async_copy(a, b, sems.at[i]) for i, (a, b) in enumerate(pairs)]
     for copy in copies:
         copy.start()
-    out_ref[...] = jnp.zeros_like(out_ref)
+    metas[...] = jnp.zeros_like(metas)
     line = lax.broadcasted_iota(jnp.int32, (META_ROWS, TILE), 0)
+    for copy in copies[:3]:
+        copy.wait()
+    coef_full[...] = coef_half[...].astype(F32)
+    spread = pltpu.make_async_copy(coef_full, coef_ref, sems.at[len(pairs)])
+    spread.start()
     slots = []
     for tile in range(TILES_DEV):
         patch, rank, before = slot_of(owner_ref, offsets_ref, tile)
@@ -123,21 +132,21 @@
                 meta = jnp.where(line == i, value.astype(F32), meta)
         meta = meta.astype(BF16)
         for parity in range(2):
-            out_ref[parity * PATCHES + patch, SLOT_ROWS:, :] = meta
-    copies[0].wait()
-    coef_full[...] = coef_half[...].astype(F32)
-    spread = pltpu.make_async_copy(coef_full, coef_ref, sems.at[5])
-    spread.start()
-    copies[1].wait()
-    copies[2].wait()
-    for first in range(0, TILES_DEV, 2):
-        side = (first // 2) % 2
-        pair = flux_ref[first : first + 2].reshape(2 * TILE, TILE)
-        rowpass[side] = jnp.dot(pair, row_ref[...], preferred_element_type=F32)
+            metas[parity * PATCHES + patch] = meta
+    sent = [
+        pltpu.make_async_copy(metas, out_hbm.at[:, pl.ds(SLOT_ROWS, META_ROWS), :], out_sems.at[0])
+    ]
+    sent[0].start()
+    copies[3].wait()
+    copies[4].wait()
+    def row_pass(pair):
+        tiles = flux_ref[2 * pair : 2 * pair + 2].reshape(2 * TILE, TILE)
+        rowpass[pair % 2] = jnp.dot(tiles, row_ref[...], preferred_element_type=F32)
+
+    def mix(pair):
+        side = pair % 2
         for part in range(2):
-            if first + part == 0:
-                spread.wait()
-            coefs = [coef_ref[first + part, k] for k in range(27)]
+            coefs = [coef_ref[2 * pair + part, k] for k in range(27)]
             for block in range(0, TILE, 16):
                 rows = slice(part * TILE + block, part * TILE + block + 16)
                 lines = [rowpass[side, rows, f * TILE : (f + 1) * TILE] for f in range(FILTERS)]
@@ -148,16 +157,17 @@
                         total = term if total is None else total + term
                     mixed[side, g * TILE + block : g * TILE + block + 16,
                           part * TILE : (part + 1) * TILE] = total.astype(BF16)
-        if first == 0:
-            copies[3].wait()
-            copies[4].wait()
-        matched = jnp.dot(col_ref[...], mixed[side], preferred_element_type=F32)
+
+    def column_pass(pair):
+        return jnp.dot(col_ref[...], mixed[pair % 2], preferred_element_type=F32)
+
+    def finish(pair, matched):
         for part in range(2):
-            tile = first + part
+            tile = 2 * pair + part
             patch, rank = slots[tile]
             weight = masked_weight(var_ref[tile], pads_ref, tile)
-            whole[side, part, 0] = weight * matched[:, part * TILE : (part + 1) * TILE]
-            whole[side, part, 1] = weight
+            whole[tile, 0] = weight * matched[:, part * TILE : (part + 1) * TILE]
+            whole[tile, 1] = weight
             for parity in range(2):
                 top = first_row(offsets_ref[0, tile], parity)
                 taken = []
@@ -166,34 +176,58 @@
                     row = (at // STRIP) * 64 + STRIP * parity + at % STRIP - offsets_ref[0, tile] * 8
                     taken.append(pl.multiple_of(row, 8))
                 for image in range(2):
-                    start = pl.multiple_of(image * CAP * 64 + rank * 64, 64)
-                    rows = [whole[side, part, image, pl.ds(row, 8), :] for row in taken]
-                    out_ref[parity * PATCHES + patch, pl.ds(start, 64), :] = jnp.concatenate(
+                    rows = [whole[tile, image, pl.ds(row, 8), :] for row in taken]
+                    halves[tile, parity, image * 64 : (image + 1) * 64, :] = jnp.concatenate(
                         rows, axis=0
                     ).astype(BF16)
+                start = pl.multiple_of(rank * TILE, TILE)
+                copy = pltpu.make_async_copy(
+                    halves.at[tile, parity],
+                    out_hbm.at[parity * PATCHES + patch, pl.ds(start, TILE), :],
+                    out_sems.at[1 + 2 * tile + parity],
+                )
+                copy.start()
+                sent.append(copy)
+
+    row_pass(0)
+    spread.wait()
+    for copy in copies[5:]:
+        copy.wait()
+    matched = None
+    for pair in range(TILES_DEV // 2):
+        if pair + 1 < TILES_DEV // 2:
+            row_pass(pair + 1)
+        mix(pair)
+        if pair > 0:
+            finish(pair - 1, matched)
+        matched = column_pass(pair)
+    finish(TILES_DEV // 2 - 1, matched)
+    for copy in sent:
+        copy.wait()
 
 
 def scatter_kernel(meta_ref, slots_ref, out_ref, images):
     images[...] = jnp.zeros_like(images)
     parity = lax.rem(lax.axis_index("group"), 2)
     lane = lax.broadcasted_iota(jnp.int32, (64, TILE), 1)
-    for source in range(2 * PATCHES):
-        for rank in range(CAP):
-
-            @pl.when(meta_ref[source, rank * 4] != 0)
-            def _():
-                row = pl.multiple_of(first_row(meta_ref[source, rank * 4 + 1], parity), 8)
-                column = meta_ref[source, rank * 4 + 2] * 8
-                block = column // TILE
-                shift = column % TILE
-                for image in range(2):
-                    start = image * CAP * 64 + rank * 64
-                    half = slots_ref[source, start : start + 64, :].astype(F32)
-                    turned = pltpu.roll(half, shift, 1)
-                    place = (image, block, pl.ds(row, 64), slice(None))
-                    images[place] += jnp.where(lane >= shift, turned, 0.0)
-                    place = (image, block + 1, pl.ds(row, 64), slice(None))
-                    images[place] += jnp.where(lane < shift, turned, 0.0)
+    for rank in range(CAP):
+        for source in range(2 * PATCHES):
+            filled = meta_ref[source, rank * 4] != 0
+            row = first_row(meta_ref[source, rank * 4 + 1], parity)
+            row = pl.multiple_of(row, 8)
+            column = meta_ref[source, rank * 4 + 2] * 8
+            block = column // TILE
+            shift = column % TILE
+            right = lane >= jnp.where(filled, shift, TILE)
+            left = lane < jnp.where(filled, shift, 0)
+            for image in range(2):
+                start = rank * TILE + image * 64
+                half = slots_ref[source, start : start + 64, :].astype(F32)
+                turned = pltpu.roll(half, shift, 1)
+                place = (image, block, pl.ds(row, 64), slice(None))
+                images[place] += jnp.where(right, turned, 0.0)
+                place = (image, block + 1, pl.ds(row, 64), slice(None))
+                images[place] += jnp.where(left, turned, 0.0)
 
     for half in range(HALF):
         for image in range(2):
@@ -238,9 +272,12 @@
         slots = pl.pallas_call(
             slot_kernel,
             out_shape=jax.ShapeDtypeStruct((2 * PATCHES, SLOT_ROWS + META_ROWS, TILE), BF16),
-            in_specs=[SMEM] * 3 + [HBM] * 5,
-            out_specs=VMEM,
+            in_specs=[HBM] * 8,
+            out_specs=HBM,
             scratch_shapes=[
+                pltpu.SMEM((1, TILES_DEV), jnp.int32),
+                pltpu.SMEM((2, TILES_DEV), jnp.int32),
+                pltpu.SMEM((4, TILES_DEV), jnp.int32),
                 pltpu.VMEM((TILES_DEV, 27), BF16),
                 pltpu.VMEM((TILES_DEV, 27), F32),
                 pltpu.SMEM((TILES_DEV, 27), F32),
@@ -250,8 +287,11 @@
                 pltpu.VMEM((TILE, FILTERS * TILE), BF16),
                 pltpu.VMEM((2, 2 * TILE, FILTERS * TILE), F32),
                 pltpu.VMEM((2, FILTERS * TILE, 2 * TILE), BF16),
-                pltpu.VMEM((2, 2, 2, TILE, TILE), F32),
-                pltpu.SemaphoreType.DMA((6,)),
+                pltpu.VMEM((TILES_DEV, 2, TILE, TILE), F32),
+                pltpu.VMEM((TILES_DEV, 2, TILE, TILE), BF16),
+                pltpu.VMEM((2 * PATCHES, META_ROWS, TILE), BF16),
+                pltpu.SemaphoreType.DMA((9,)),
+                pltpu.SemaphoreType.DMA((1 + 2 * TILES_DEV,)),
             ],
             compiler_params=pltpu.CompilerParams(vmem_limit_bytes=VMEM_ALL),
         )(

time: 88.8 us -> 87.1 us (0.981)
  the two profiles are of different devices: /device:TPU:1 before, /device:TPU:2 now
where the time goes in v3:
time: 87.1 us; the launch traced here: 86.8 us
  blocking collectives  78.8 us (90%)
  Pallas kernels  7.2 us (8%)
    all_to_all x1, blocking collectives, on_device(): lax.all_to_all(strips, 'group', 0, 0, tiled=True, axis_index_groups=parit...  46.5 us
    all_to_all x1, blocking collectives, on_device(): lax.all_to_all(slots, ('group', 'patch'), 0, 0, tiled=True, axis_index_gr...  23.2 us
    all_to_all x1, blocking collectives, on_device(): chi_parts = lax.all_to_all(chi_copies, 'band', 0, 0, tiled=True)  9.14 us
    pallas_call x1, Pallas kernels, on_device(): pl.pallas_call(slot_kernel, out_shape=jax.ShapeDtypeStruct((2 * PATCHES,...  4.49 us

profile of v3, /device:TPU:2, one launch (start us, length us, event | category | flops | bytes accessed | tf_op | source)
XLA Modules:
  0.0 86.8 jit_solution(9374517664981162899)
XLA Ops:
  0.6 4.5 %tile_slots.1 = bf16[16,272,128]{2,1,0:T(8,128)(2,1)} custom-call(s32[1,8]{1,0:T(1,128)} %bitcast.21, s32[2,8]{1,0:T(2,128)} %bitcast.20, s32[4,8]{1,0:T(4,128)} %bitcast.18, bf16[8,27]{1,0:T(8,128)(2,1)} %bitcast.19, bf16[8,128,128]{2,1,0:T(8,128)(2,1)} %bitcast.15, bf16[8,128,128]{2,1,0:T(8,128)(2,1)} %bitcast.16, ...), custom_call_target="tpu_custom_call" | custom-call | tf_op jit(solution)/shard_map/tile_slots/pallas_call | solution.py:272
  5.1 23.2 %all_to_all.15.slots_ref = bf16[16,272,128]{2,1,0:T(8,128)(2,1)S(1)} all-to-all(bf16[16,272,128]{2,1,0:T(8,128)(2,1)} %tile_slots.1), channel_id=1, replica_groups={{0,1,2,3,4,5,6,7,8,9,10,11,12,13,14,15},{16,17,18,19,20,21,22,23,24,25,..., dimensions={0} | all-to-all | bytes 2228224 | tf_op jit(solution)/shard_map/all_to_all | solution.py:311
  28.3 0.2 copy.14
  28.5 1.4 %strip_images.1 = bf16[8,2,32,512]{3,2,1,0:T(8,128)(2,1)S(1)} custom-call(s32[16,8]{1,0:T(8,128)S(1)} %bitcast.14, bf16[16,272,128]{2,1,0:T(8,128)(2,1)S(1)} %all_to_all.15.slots_ref), custom_call_target="tpu_custom_call" | custom-call | tf_op jit(solution)/shard_map/strip_images/pallas_call | solution.py:316
  29.8 46.5 %all_to_all.16.strips_ref = bf16[8,2,32,512]{3,2,1,0:T(8,128)(2,1)S(1)} all-to-all(bf16[8,2,32,512]{3,2,1,0:T(8,128)(2,1)S(1)} %strip_images.1), channel_id=1, replica_groups={{0,16,32,48,64,80,96,112},{8,24,40,56,72,88,104,120},{1,17,33,49,65,81,..., dimensions={0} | all-to-all | bytes 1048576 | tf_op jit(solution)/shard_map/all_to_all | solution.py:325
  76.3 0.7 strip_sums.1
  77.0 9.1 %all_to_all.17.parts_ref = bf16[4,32,512]{2,1,0:T(8,128)(2,1)S(1)} all-to-all(bf16[4,32,512]{2,1,0:T(8,128)(2,1)S(1)} %get-tuple-element.5), channel_id=1, replica_groups=mesh['band'=4,'group'=16,'patch'=8] {'band'}, dimensions={0} | all-to-all | bytes 262144 | tf_op jit(solution)/shard_map/all_to_all | solution.py:337
  86.2 0.6 chi_sum.1
  (1 shorter events, 0.0 us)

commit v4 on v3

--- a/solution.py
+++ b/solution.py
@@ -65,20 +65,28 @@
 TERM_LIST = term_list()
 
 
-def slot_of(owner_ref, offsets_ref, tile):
-    patch = owner_ref[0, tile]
-    rank = jnp.int32(0)
-    before = [jnp.int32(0), jnp.int32(0)]
-    for other in range(tile):
-        same = owner_ref[0, other] == patch
-        rank = rank + jnp.where(same, 1, 0)
-        before = [v + jnp.where(same, offsets_ref[i, other], 0) for i, v in enumerate(before)]
-    return patch, rank, before
+def slots_of(owner_ref, offsets_ref):
+    patches = [owner_ref[0, tile] for tile in range(TILES_DEV)]
+    codes = [(1 << 16) + (offsets_ref[0, t] << 8) + offsets_ref[1, t] for t in range(TILES_DEV)]
+    slots = []
+    for tile in range(TILES_DEV):
+        seen = jnp.int32(0)
+        for other in range(tile):
+            seen = seen + jnp.where(patches[other] == patches[tile], codes[other], 0)
+        slots.append((patches[tile], seen >> 16, (seen >> 8) & 255, seen & 255))
+    return slots
 
 
 def first_row(row_offset, parity):
     row = row_offset * 8
-    return (row // 64) * STRIP + jnp.clip(row % 64 - STRIP * parity, 0, STRIP)
+    return (row >> 6) * STRIP + jnp.clip((row & 63) - STRIP * parity, 0, STRIP)
+
+
+def rows_of_parity(row_offset, parity):
+    ahead = (4 * parity - row_offset) & 7
+    cut = jnp.where(ahead > 4, 8 - ahead, 0)
+    start = jnp.where(ahead > 4, 0, ahead * 8)
+    return [pl.multiple_of(start + 8 * i + (((cut + i) >> 2) << 5), 8) for i in range(4)]
 
 
 def masked_weight(var_tile, pads_ref, tile):
@@ -118,23 +126,27 @@
     coef_full[...] = coef_half[...].astype(F32)
     spread = pltpu.make_async_copy(coef_full, coef_ref, sems.at[len(pairs)])
     spread.start()
-    slots = []
+    slots = slots_of(owner_ref, offsets_ref)
     for tile in range(TILES_DEV):
-        patch, rank, before = slot_of(owner_ref, offsets_ref, tile)
-        slots.append((patch, rank))
-        now = [offsets_ref[0, tile], offsets_ref[1, tile]]
+        patch, rank, row_before, col_before = slots[tile]
+        row_now, col_now = offsets_ref[0, tile], offsets_ref[1, tile]
         second = rank > 0
-        entry = [jnp.int32(1)] + [jnp.where(second, u, v) for u, v in zip(before, now)]
-        entry = entry + [jnp.int32(0), rank] + [jnp.where(second, v, 0) for v in now]
-        meta = jnp.zeros((META_ROWS, TILE), F32)
-        for i, value in enumerate(entry):
-            if i != 3:
-                meta = jnp.where(line == i, value.astype(F32), meta)
-        meta = meta.astype(BF16)
+        entry = {
+            0: jnp.int32(1),
+            1: jnp.where(second, row_before, row_now),
+            2: jnp.where(second, col_before, col_now),
+            4: rank,
+            5: jnp.where(second, row_now, 0),
+            6: jnp.where(second, col_now, 0),
+        }
+        meta = jnp.zeros((META_ROWS, TILE), jnp.int32)
+        for i, value in entry.items():
+            meta = jnp.where(line == i, value, meta)
+        meta = meta.astype(F32).astype(BF16)
         for parity in range(2):
-            metas[parity * PATCHES + patch] = meta
+            metas[parity, patch] = meta
     sent = [
-        pltpu.make_async_copy(metas, out_hbm.at[:, pl.ds(SLOT_ROWS, META_ROWS), :], out_sems.at[0])
+        pltpu.make_async_copy(metas, out_hbm.at[:, :, pl.ds(SLOT_ROWS, META_ROWS), :], out_sems.at[0])
     ]
     sent[0].start()
     copies[3].wait()
@@ -164,30 +176,26 @@
     def finish(pair, matched):
         for part in range(2):
             tile = 2 * pair + part
-            patch, rank = slots[tile]
+            patch, rank = slots[tile][:2]
             weight = masked_weight(var_ref[tile], pads_ref, tile)
             whole[tile, 0] = weight * matched[:, part * TILE : (part + 1) * TILE]
             whole[tile, 1] = weight
             for parity in range(2):
-                top = first_row(offsets_ref[0, tile], parity)
-                taken = []
-                for group in range(8):
-                    at = top + 8 * group
-                    row = (at // STRIP) * 64 + STRIP * parity + at % STRIP - offsets_ref[0, tile] * 8
-                    taken.append(pl.multiple_of(row, 8))
+                taken = rows_of_parity(offsets_ref[0, tile], parity)
+                taken = taken + [pl.multiple_of(row + 64, 8) for row in taken]
                 for image in range(2):
                     rows = [whole[tile, image, pl.ds(row, 8), :] for row in taken]
                     halves[tile, parity, image * 64 : (image + 1) * 64, :] = jnp.concatenate(
                         rows, axis=0
                     ).astype(BF16)
-                start = pl.multiple_of(rank * TILE, TILE)
-                copy = pltpu.make_async_copy(
-                    halves.at[tile, parity],
-                    out_hbm.at[parity * PATCHES + patch, pl.ds(start, TILE), :],
-                    out_sems.at[1 + 2 * tile + parity],
-                )
-                copy.start()
-                sent.append(copy)
+            start = pl.multiple_of(rank * TILE, TILE)
+            copy = pltpu.make_async_copy(
+                halves.at[tile],
+                out_hbm.at[:, patch, pl.ds(start, TILE), :],
+                out_sems.at[1 + tile],
+            )
+            copy.start()
+            sent.append(copy)
 
     row_pass(0)
     spread.wait()
@@ -216,8 +224,8 @@
             row = first_row(meta_ref[source, rank * 4 + 1], parity)
             row = pl.multiple_of(row, 8)
             column = meta_ref[source, rank * 4 + 2] * 8
-            block = column // TILE
-            shift = column % TILE
+            block = column >> 7
+            shift = column & (TILE - 1)
             right = lane >= jnp.where(filled, shift, TILE)
             left = lane < jnp.where(filled, shift, 0)
             for image in range(2):
@@ -271,7 +279,7 @@
     with jax.named_scope("tile_slots"):
         slots = pl.pallas_call(
             slot_kernel,
-            out_shape=jax.ShapeDtypeStruct((2 * PATCHES, SLOT_ROWS + META_ROWS, TILE), BF16),
+            out_shape=jax.ShapeDtypeStruct((2, PATCHES, SLOT_ROWS + META_ROWS, TILE), BF16),
             in_specs=[HBM] * 8,
             out_specs=HBM,
             scratch_shapes=[
@@ -289,9 +297,9 @@
                 pltpu.VMEM((2, FILTERS * TILE, 2 * TILE), BF16),
                 pltpu.VMEM((TILES_DEV, 2, TILE, TILE), F32),
                 pltpu.VMEM((TILES_DEV, 2, TILE, TILE), BF16),
-                pltpu.VMEM((2 * PATCHES, META_ROWS, TILE), BF16),
+                pltpu.VMEM((2, PATCHES, META_ROWS, TILE), BF16),
                 pltpu.SemaphoreType.DMA((9,)),
-                pltpu.SemaphoreType.DMA((1 + 2 * TILES_DEV,)),
+                pltpu.SemaphoreType.DMA((1 + TILES_DEV,)),
             ],
             compiler_params=pltpu.CompilerParams(vmem_limit_bytes=VMEM_ALL),
         )(
@@ -304,6 +312,7 @@
             jnp.asarray(row_table),
             jnp.asarray(column_table),
         )
+    slots = slots.reshape((2 * PATCHES,) + slots.shape[2:])
     blocks = [
         [z * PATCHES + patch for z in (low, low + 1) for patch in range(PATCHES)]
         for low in range(0, STRIPS, 2)

time: 87.1 us -> 86.5 us (level)
  no operation moved by 1% of the time
where the time goes in v4:
time: 86.5 us; the launch traced here: 86.3 us
  blocking collectives  78.8 us (91%)
  Pallas kernels  6.63 us (8%)
    all_to_all x1, blocking collectives, on_device(): lax.all_to_all(strips, 'group', 0, 0, tiled=True, axis_index_groups=parit...  46.5 us
    all_to_all x1, blocking collectives, on_device(): lax.all_to_all(slots, ('group', 'patch'), 0, 0, tiled=True, axis_index_gr...  23.2 us
    all_to_all x1, blocking collectives, on_device(): chi_parts = lax.all_to_all(chi_copies, 'band', 0, 0, tiled=True)  9.14 us
    pallas_call x1, Pallas kernels, on_device(): pl.pallas_call(slot_kernel, out_shape=jax.ShapeDtypeStruct((2, PATCHES, S...  3.97 us

profile of v4, /device:TPU:2, one launch (start us, length us, event | category | flops | bytes accessed | tf_op | source)
XLA Modules:
  0.0 86.3 jit_solution(604338282198788488)
XLA Ops:
  0.6 4.0 %tile_slots.1 = bf16[2,8,272,128]{3,2,1,0:T(8,128)(2,1)} custom-call(s32[1,8]{1,0:T(1,128)} %bitcast.23, s32[2,8]{1,0:T(2,128)} %bitcast.22, s32[4,8]{1,0:T(4,128)} %bitcast.20, bf16[8,27]{1,0:T(8,128)(2,1)} %bitcast.21, bf16[8,128,128]{2,1,0:T(8,128)(2,1)} %bitcast.17, bf16[8,128,128]{2,1,0:T(8,128)(2,1)} %bitcast.18, ...), custom_call_target="tpu_custom_call" | custom-call | tf_op jit(solution)/shard_map/tile_slots/pallas_call | solution.py:280
  4.6 23.2 %all_to_all.15.slots_ref = bf16[16,272,128]{2,1,0:T(8,128)(2,1)S(1)} all-to-all(bf16[16,272,128]{2,1,0:T(8,128)(2,1)} %bitcast.16), channel_id=1, replica_groups={{0,1,2,3,4,5,6,7,8,9,10,11,12,13,14,15},{16,17,18,19,20,21,22,23,24,25,..., dimensions={0} | all-to-all | bytes 2228224 | tf_op jit(solution)/shard_map/all_to_all | solution.py:320
  27.8 0.2 copy.14
  27.9 1.3 %strip_images.1 = bf16[8,2,32,512]{3,2,1,0:T(8,128)(2,1)S(1)} custom-call(s32[16,8]{1,0:T(8,128)S(1)} %bitcast.15, bf16[16,272,128]{2,1,0:T(8,128)(2,1)S(1)} %all_to_all.15.slots_ref), custom_call_target="tpu_custom_call" | custom-call | tf_op jit(solution)/shard_map/strip_images/pallas_call | solution.py:325
  29.3 46.5 %all_to_all.16.strips_ref = bf16[8,2,32,512]{3,2,1,0:T(8,128)(2,1)S(1)} all-to-all(bf16[8,2,32,512]{3,2,1,0:T(8,128)(2,1)S(1)} %strip_images.1), channel_id=1, replica_groups={{0,16,32,48,64,80,96,112},{8,24,40,56,72,88,104,120},{1,17,33,49,65,81,..., dimensions={0} | all-to-all | bytes 1048576 | tf_op jit(solution)/shard_map/all_to_all | solution.py:334
  75.8 0.7 strip_sums.1
  76.5 9.1 %all_to_all.17.parts_ref = bf16[4,32,512]{2,1,0:T(8,128)(2,1)S(1)} all-to-all(bf16[4,32,512]{2,1,0:T(8,128)(2,1)S(1)} %get-tuple-element.5), channel_id=1, replica_groups=mesh['band'=4,'group'=16,'patch'=8] {'band'}, dimensions={0} | all-to-all | bytes 262144 | tf_op jit(solution)/shard_map/all_to_all | solution.py:346
  85.6 0.6 chi_sum.1
  (1 shorter events, 0.0 us)

commit v5 on v4

--- a/solution.py
+++ b/solution.py
@@ -21,7 +21,7 @@
 SLOT_ROWS = 2 * CAP * 64
 STRIP = 32
 STRIPS = PATCH_SIDE // STRIP
-HALF = STRIPS // 2
+QUARTER = STRIPS // 4
 COL_BLOCKS = PATCH_SIDE // TILE
 F32 = jnp.float32
 BF16 = jnp.bfloat16
@@ -214,7 +214,7 @@
         copy.wait()
 
 
-def scatter_kernel(meta_ref, slots_ref, out_ref, images):
+def scatter_kernel(meta_ref, slots_ref, keep_ref, send_ref, images):
     images[...] = jnp.zeros_like(images)
     parity = lax.rem(lax.axis_index("group"), 2)
     lane = lax.broadcasted_iota(jnp.int32, (64, TILE), 1)
@@ -237,20 +237,33 @@
                 place = (image, block + 1, pl.ds(row, 64), slice(None))
                 images[place] += jnp.where(left, turned, 0.0)
 
-    for half in range(HALF):
+    own = (lax.axis_index("group") >> 1) & 1
+    for entry in range(QUARTER):
+        kept = pl.multiple_of((2 * entry + own) * STRIP, STRIP)
+        sent = pl.multiple_of((2 * entry + 1 - own) * STRIP, STRIP)
         for image in range(2):
             for block in range(COL_BLOCKS):
-                out_ref[half, image, :, block * TILE : (block + 1) * TILE] = images[
-                    image, block, half * STRIP : (half + 1) * STRIP, :
+                columns = slice(block * TILE, (block + 1) * TILE)
+                keep_ref[entry, image, :, columns] = images[image, block, pl.ds(kept, STRIP), :]
+                send_ref[entry, image, :, columns] = images[
+                    image, block, pl.ds(sent, STRIP), :
                 ].astype(BF16)
 
 
-def reduce_kernel(strips_ref, coadd_ref, chi_ref):
-    flux = strips_ref[0, 0].astype(F32)
-    weight = strips_ref[0, 1].astype(F32)
-    for half in range(1, HALF):
-        flux = flux + strips_ref[half, 0].astype(F32)
-        weight = weight + strips_ref[half, 1].astype(F32)
+def quad_kernel(keep_ref, got_ref, own_ref, *out_refs):
+    here = lax.axis_index("group") >> 2
+    own_ref[...] = keep_ref[here] + got_ref[here].astype(F32)
+    for step, out_ref in enumerate(out_refs, 1):
+        entry = (here + step) & (QUARTER - 1)
+        out_ref[...] = (keep_ref[entry] + got_ref[entry].astype(F32)).astype(BF16)
+
+
+def reduce_kernel(own_ref, *refs):
+    strip_refs, (coadd_ref, chi_ref) = refs[:-2], refs[-2:]
+    flux, weight = own_ref[0], own_ref[1]
+    for strip_ref in strip_refs:
+        flux = flux + strip_ref[0].astype(F32)
+        weight = weight + strip_ref[1].astype(F32)
     coadd = flux / (weight + 1.0)
     coadd_ref[...] = coadd
     chi = (flux * coadd).astype(BF16)
@@ -322,16 +335,36 @@
     )
     meta = slots_got[:, SLOT_ROWS : SLOT_ROWS + 8, 0].astype(jnp.int32)
     with jax.named_scope("strip_images"):
-        strips = pl.pallas_call(
+        kept, sent = pl.pallas_call(
             scatter_kernel,
-            out_shape=jax.ShapeDtypeStruct((HALF, 2, STRIP, PATCH_SIDE), BF16),
+            out_shape=(
+                jax.ShapeDtypeStruct((QUARTER, 2, STRIP, PATCH_SIDE), F32),
+                jax.ShapeDtypeStruct((QUARTER, 2, STRIP, PATCH_SIDE), BF16),
+            ),
             in_specs=[SMEM, VMEM],
-            out_specs=VMEM,
+            out_specs=(VMEM, VMEM),
             scratch_shapes=[pltpu.VMEM((2, COL_BLOCKS + 1, PATCH_SIDE // 2, TILE), F32)],
             compiler_params=PARAMS,
         )(meta, slots_got)
-    parities = [list(range(parity, STRIPS, 2)) for parity in range(2)]
-    strips_got = lax.all_to_all(strips, "group", 0, 0, tiled=True, axis_index_groups=parities)
+    pairs = []
+    for z in range(STRIPS):
+        for patch in range(PATCHES):
+            shift = 2 if (z >> 1) % 2 == patch % 2 else -2
+            pairs.append((z * PATCHES + patch, (z + shift) % STRIPS * PATCHES + patch))
+    got = lax.ppermute(sent, ("group", "patch"), pairs)
+    with jax.named_scope("quad_sums"):
+        quads = pl.pallas_call(
+            quad_kernel,
+            out_shape=(jax.ShapeDtypeStruct((2, STRIP, PATCH_SIDE), F32),)
+            + (jax.ShapeDtypeStruct((2, STRIP, PATCH_SIDE), BF16),) * (QUARTER - 1),
+            in_specs=[VMEM, VMEM],
+            out_specs=(VMEM,) * QUARTER,
+            compiler_params=PARAMS,
+        )(kept, got)
+    strips_got = [quads[0]]
+    for step in (2,1,3):
+        ring = [(z, (z + 4 * step) % STRIPS) for z in range(STRIPS)]
+        strips_got.append(lax.ppermute(quads[step], "group", ring))
     with jax.named_scope("strip_sums"):
         coadd, chi_copies = pl.pallas_call(
             reduce_kernel,
@@ -339,10 +372,10 @@
                 jax.ShapeDtypeStruct((STRIP, PATCH_SIDE), F32),
                 jax.ShapeDtypeStruct((bands, STRIP, PATCH_SIDE), BF16),
             ),
-            in_specs=[VMEM],
+            in_specs=[VMEM] * QUARTER,
             out_specs=(VMEM, VMEM),
             compiler_params=PARAMS,
-        )(strips_got)
+        )(*strips_got)
     chi_parts = lax.all_to_all(chi_copies, "band", 0, 0, tiled=True)
     with jax.named_scope("chi_sum"):
         chi = pl.pallas_call(

time: 86.5 us -> 84 us (0.971)
  the two profiles are of different devices: /device:TPU:2 before, /device:TPU:1 now
where the time goes in v5:
time: 84 us; the launch traced here: 83.7 us
  blocking collectives  34.5 us (41%)
  starting transfers between devices  26.2 us (31%)
  waiting for transfers between devices  15.4 us (18%)
  Pallas kernels  6.63 us (8%)
    all_to_all x1, blocking collectives, on_device(): lax.all_to_all(slots, ('group', 'patch'), 0, 0, tiled=True, axis_index_gr...  27.3 us
    ppermute x3, starting transfers between devices, on_device(): strips_got.append(lax.ppermute(quads[step], 'group', ring))  18.6 us
    ppermute x3, waiting for transfers between devices, on_device(): strips_got.append(lax.ppermute(quads[step], 'group', ring))  9.76 us
    ppermute x1, starting transfers between devices, on_device(): got = lax.ppermute(sent, ('group', 'patch'), pairs)  7.58 us
    all_to_all x1, blocking collectives, on_device(): chi_parts = lax.all_to_all(chi_copies, 'band', 0, 0, tiled=True)  7.21 us
    ppermute x1, waiting for transfers between devices, on_device(): got = lax.ppermute(sent, ('group', 'patch'), pairs)  5.66 us
    pallas_call x1, Pallas kernels, on_device(): pl.pallas_call(slot_kernel, out_shape=jax.ShapeDtypeStruct((2, PATCHES, S...  3.97 us
  transfers between devices with their start and end apart: 4, of which 3 were waited for; matrix products, arithmetic and copies ran while one was open for 0% of the time, Pallas kernels for 0%

profile of v5, /device:TPU:1, one launch (start us, length us, event | category | flops | bytes accessed | tf_op | source)
XLA Modules:
  0.0 83.7 jit_solution(9767423190107718157)
XLA Ops:
  0.6 4.0 %tile_slots.1 = bf16[2,8,272,128]{3,2,1,0:T(8,128)(2,1)} custom-call(s32[1,8]{1,0:T(1,128)} %bitcast.23, s32[2,8]{1,0:T(2,128)} %bitcast.22, s32[4,8]{1,0:T(4,128)} %bitcast.20, bf16[8,27]{1,0:T(8,128)(2,1)} %bitcast.21, bf16[8,128,128]{2,1,0:T(8,128)(2,1)} %bitcast.17, bf16[8,128,128]{2,1,0:T(8,128)(2,1)} %bitcast.18, ...), custom_call_target="tpu_custom_call" | custom-call | tf_op jit(solution)/shard_map/tile_slots/pallas_call | solution.py:293
  4.6 27.3 %all_to_all.10.slots_ref = bf16[16,272,128]{2,1,0:T(8,128)(2,1)S(1)} all-to-all(bf16[16,272,128]{2,1,0:T(8,128)(2,1)} %bitcast.16), channel_id=1, replica_groups={{0,1,2,3,4,5,6,7,8,9,10,11,12,13,14,15},{16,17,18,19,20,21,22,23,24,25,..., dimensions={0} | all-to-all | bytes 2228224 | tf_op jit(solution)/shard_map/all_to_all | solution.py:333
  31.9 0.2 copy.14
  32.1 1.3 %strip_images.1 = (f32[4,2,32,512]{3,2,1,0:T(8,128)S(1)}, bf16[4,2,32,512]{3,2,1,0:T(8,128)(2,1)S(1)}) custom-call(s32[16,8]{1,0:T(8,128)S(1)} %bitcast.15, bf16[16,272,128]{2,1,0:T(8,128)(2,1)S(1)} %all_to_all.10.slots_ref), custom_call_target="tpu_custom_call" | custom-call | tf_op jit(solution)/shard_map/strip_images/pallas_call | solution.py:338
  33.4 7.6 %collective-permute-start = (bf16[4,2,32,512]{3,2,1,0:T(8,128)(2,1)S(1)}, bf16[4,2,32,512]{3,2,1,0:T(8,128)(2,1)S(1)}, u32[]{:S(2)}, u32[]{:S(2)}) collective-permute-start(bf16[4,2,32,512]{3,2,1,0:T(8,128)(2,1)S(1)} %get-tuple-element.11), channel_id=1, source_target_pairs={{0,16},{1,113},{2,18},{3,115},{4,20},{5,117},{6,22},{7,119},{8,24}... | collective-permute-start | bytes 786440 | tf_op jit(solution)/shard_map/ppermute | solution.py:354
  41.0 5.7 %collective-permute-done.got_ref = bf16[4,2,32,512]{3,2,1,0:T(8,128)(2,1)S(1)} collective-permute-done((bf16[4,2,32,512]{3,2,1,0:T(8,128)(2,1)S(1)}, bf16[4,2,32,512]{3,2,1,0:T(8,128)(2,1)S(1)}, u32[]{:S(2)}, u32[]{:S(2)}) %collective-permute-start) | collective-permute-done | bytes 262176 | tf_op jit(solution)/shard_map/ppermute | solution.py:354
  46.7 9.4 %collective-permute-start.1 = (bf16[2,32,512]{2,1,0:T(8,128)(2,1)S(1)}, bf16[2,32,512]{2,1,0:T(8,128)(2,1)S(1)}, u32[]{:S(2)}, u32[]{:S(2)}) collective-permute-start(bf16[2,32,512]{2,1,0:T(8,128)(2,1)S(1)} %get-tuple-element.13), channel_id=1, source_target_pairs={{0,64},{8,72},{16,80},{24,88},{32,96},{40,104},{48,112},{56,120},{... | collective-permute-start | bytes 196616 | tf_op jit(solution)/shard_map/ppermute | solution.py:367
  56.1 4.9 %collective-permute-start.2 = (bf16[2,32,512]{2,1,0:T(8,128)(2,1)S(1)}, bf16[2,32,512]{2,1,0:T(8,128)(2,1)S(1)}, u32[]{:S(2)}, u32[]{:S(2)}) collective-permute-start(bf16[2,32,512]{2,1,0:T(8,128)(2,1)S(1)} %get-tuple-element.14), channel_id=1, source_target_pairs={{0,32},{8,40},{16,48},{24,56},{32,64},{40,72},{48,80},{56,88},{64,... | collective-permute-start | bytes 196616 | tf_op jit(solution)/shard_map/ppermute | solution.py:367
  61.0 4.3 %collective-permute-start.3 = (bf16[2,32,512]{2,1,0:T(8,128)(2,1)S(1)}, bf16[2,32,512]{2,1,0:T(8,128)(2,1)S(1)}, u32[]{:S(2)}, u32[]{:S(2)}) collective-permute-start(bf16[2,32,512]{2,1,0:T(8,128)(2,1)S(1)} %get-tuple-element.15), channel_id=1, source_target_pairs={{0,96},{8,104},{16,112},{24,120},{32,0},{40,8},{48,16},{56,24},{64... | collective-permute-start | bytes 196616 | tf_op jit(solution)/shard_map/ppermute | solution.py:367
  65.4 0.0 collective-permute-done.1.refs_0_
  65.4 0.1 collective-permute-done.2.refs_1_
  65.5 9.6 %collective-permute-done.3.refs_2_ = bf16[2,32,512]{2,1,0:T(8,128)(2,1)S(1)} collective-permute-done((bf16[2,32,512]{2,1,0:T(8,128)(2,1)S(1)}, bf16[2,32,512]{2,1,0:T(8,128)(2,1)S(1)}, u32[]{:S(2)}, u32[]{:S(2)}) %collective-permute-start.3) | collective-permute-done | bytes 65568 | tf_op jit(solution)/shard_map/ppermute | solution.py:367
  75.1 0.7 strip_sums.1
  75.8 7.2 %all_to_all.11.parts_ref = bf16[4,32,512]{2,1,0:T(8,128)(2,1)S(1)} all-to-all(bf16[4,32,512]{2,1,0:T(8,128)(2,1)S(1)} %get-tuple-element.17), channel_id=1, replica_groups=mesh['band'=4,'group'=16,'patch'=8] {'band'}, dimensions={0} | all-to-all | bytes 262144 | tf_op jit(solution)/shard_map/all_to_all | solution.py:379
  83.0 0.6 chi_sum.1
  (2 shorter events, 0.1 us)
Async XLA Ops:
  33.4 13.3 %collective-permute-start = (bf16[4,2,32,512]{3,2,1,0:T(8,128)(2,1)S(1)}, bf16[4,2,32,512]{3,2,1,0:T(8,128)(2,1)S(1)}, u32[]{:S(2)}, u32[]{:S(2)}) collective-permute-start(bf16[4,2,32,512]{3,2,1,0:T(8,128)(2,1)S(1)} %get-tuple-element.11), channel_id=1, source_target_pairs={{0,16},{1,113},{2,18},{3,115},{4,20},{5,117},{6,22},{7,119},{8,24}... | collective-permute-start | bytes 786440 | tf_op jit(solution)/shard_map/ppermute | solution.py:354
  46.7 18.7 %collective-permute-start.1 = (bf16[2,32,512]{2,1,0:T(8,128)(2,1)S(1)}, bf16[2,32,512]{2,1,0:T(8,128)(2,1)S(1)}, u32[]{:S(2)}, u32[]{:S(2)}) collective-permute-start(bf16[2,32,512]{2,1,0:T(8,128)(2,1)S(1)} %get-tuple-element.13), channel_id=1, source_target_pairs={{0,64},{8,72},{16,80},{24,88},{32,96},{40,104},{48,112},{56,120},{... | collective-permute-start | bytes 196616 | tf_op jit(solution)/shard_map/ppermute | solution.py:367
  56.1 9.4 %collective-permute-start.2 = (bf16[2,32,512]{2,1,0:T(8,128)(2,1)S(1)}, bf16[2,32,512]{2,1,0:T(8,128)(2,1)S(1)}, u32[]{:S(2)}, u32[]{:S(2)}) collective-permute-start(bf16[2,32,512]{2,1,0:T(8,128)(2,1)S(1)} %get-tuple-element.14), channel_id=1, source_target_pairs={{0,32},{8,40},{16,48},{24,56},{32,64},{40,72},{48,80},{56,88},{64,... | collective-permute-start | bytes 196616 | tf_op jit(solution)/shard_map/ppermute | solution.py:367
  61.0 14.1 %collective-permute-start.3 = (bf16[2,32,512]{2,1,0:T(8,128)(2,1)S(1)}, bf16[2,32,512]{2,1,0:T(8,128)(2,1)S(1)}, u32[]{:S(2)}, u32[]{:S(2)}) collective-permute-start(bf16[2,32,512]{2,1,0:T(8,128)(2,1)S(1)} %get-tuple-element.15), channel_id=1, source_target_pairs={{0,96},{8,104},{16,112},{24,120},{32,0},{40,8},{48,16},{56,24},{64... | collective-permute-start | bytes 196616 | tf_op jit(solution)/shard_map/ppermute | solution.py:367

commit v6 on v5

--- a/solution.py
+++ b/solution.py
@@ -271,11 +271,12 @@
         chi_ref[band] = chi
 
 
-def chi_kernel(parts_ref, out_ref):
+def chi_kernel(coadd_ref, parts_ref, coadd_out, chi_out):
+    coadd_out[...] = coadd_ref[...]
     total = parts_ref[0].astype(F32)
     for band in range(1, parts_ref.shape[0]):
         total = total + parts_ref[band].astype(F32)
-    out_ref[...] = total
+    chi_out[...] = total
 
 
 SMEM = pl.BlockSpec(memory_space=pltpu.SMEM)
@@ -378,13 +379,13 @@
         )(*strips_got)
     chi_parts = lax.all_to_all(chi_copies, "band", 0, 0, tiled=True)
     with jax.named_scope("chi_sum"):
-        chi = pl.pallas_call(
+        coadd, chi = pl.pallas_call(
             chi_kernel,
-            out_shape=jax.ShapeDtypeStruct((STRIP, PATCH_SIDE), F32),
-            in_specs=[VMEM],
-            out_specs=VMEM,
+            out_shape=(jax.ShapeDtypeStruct((STRIP, PATCH_SIDE), F32),) * 2,
+            in_specs=[VMEM, VMEM],
+            out_specs=(VMEM, VMEM),
             compiler_params=PARAMS,
-        )(chi_parts)
+        )(coadd, chi_parts)
     return (coadd[None, None], chi[None])
 
 

time: 84 us -> 83.3 us (level)
  no operation moved by 1% of the time
where the time goes in v6:
time: 83.3 us; the launch traced here: 83 us
  blocking collectives  34.5 us (41%)
  starting transfers between devices  26.2 us (31%)
  waiting for transfers between devices  15.3 us (18%)
  Pallas kernels  6.03 us (7%)
    all_to_all x1, blocking collectives, on_device(): lax.all_to_all(slots, ('group', 'patch'), 0, 0, tiled=True, axis_index_gr...  27.3 us
    ppermute x3, starting transfers between devices, on_device(): strips_got.append(lax.ppermute(quads[step], 'group', ring))  18.6 us
    ppermute x3, waiting for transfers between devices, on_device(): strips_got.append(lax.ppermute(quads[step], 'group', ring))  9.68 us
    ppermute x1, starting transfers between devices, on_device(): got = lax.ppermute(sent, ('group', 'patch'), pairs)  7.6 us
    all_to_all x1, blocking collectives, on_device(): chi_parts = lax.all_to_all(chi_copies, 'band', 0, 0, tiled=True)  7.22 us
    ppermute x1, waiting for transfers between devices, on_device(): got = lax.ppermute(sent, ('group', 'patch'), pairs)  5.66 us
    pallas_call x1, Pallas kernels, on_device(): pl.pallas_call(slot_kernel, out_shape=jax.ShapeDtypeStruct((2, PATCHES, S...  3.98 us
  transfers between devices with their start and end apart: 4, of which 3 were waited for; matrix products, arithmetic and copies ran while one was open for 0% of the time, Pallas kernels for 0%

profile of v6, /device:TPU:1, one launch (start us, length us, event | category | flops | bytes accessed | tf_op | source)
XLA Modules:
  0.0 83.0 jit_solution(13433816833249091690)
XLA Ops:
  0.6 4.0 %tile_slots.1 = bf16[2,8,272,128]{3,2,1,0:T(8,128)(2,1)} custom-call(s32[1,8]{1,0:T(1,128)} %bitcast.22, s32[2,8]{1,0:T(2,128)} %bitcast.21, s32[4,8]{1,0:T(4,128)} %bitcast.19, bf16[8,27]{1,0:T(8,128)(2,1)} %bitcast.20, bf16[8,128,128]{2,1,0:T(8,128)(2,1)} %bitcast.17, bf16[8,128,128]{2,1,0:T(8,128)(2,1)} %bitcast.18, ...), custom_call_target="tpu_custom_call" | custom-call | tf_op jit(solution)/shard_map/tile_slots/pallas_call | solution.py:294
  4.6 27.3 %all_to_all.10.slots_ref = bf16[16,272,128]{2,1,0:T(8,128)(2,1)S(1)} all-to-all(bf16[16,272,128]{2,1,0:T(8,128)(2,1)} %bitcast.16), channel_id=1, replica_groups={{0,1,2,3,4,5,6,7,8,9,10,11,12,13,14,15},{16,17,18,19,20,21,22,23,24,25,..., dimensions={0} | all-to-all | bytes 2228224 | tf_op jit(solution)/shard_map/all_to_all | solution.py:334
  31.9 0.2 copy.14
  32.1 1.3 %strip_images.1 = (f32[4,2,32,512]{3,2,1,0:T(8,128)S(1)}, bf16[4,2,32,512]{3,2,1,0:T(8,128)(2,1)S(1)}) custom-call(s32[16,8]{1,0:T(8,128)S(1)} %bitcast.15, bf16[16,272,128]{2,1,0:T(8,128)(2,1)S(1)} %all_to_all.10.slots_ref), custom_call_target="tpu_custom_call" | custom-call | tf_op jit(solution)/shard_map/strip_images/pallas_call | solution.py:339
  33.4 7.6 %collective-permute-start = (bf16[4,2,32,512]{3,2,1,0:T(8,128)(2,1)S(1)}, bf16[4,2,32,512]{3,2,1,0:T(8,128)(2,1)S(1)}, u32[]{:S(2)}, u32[]{:S(2)}) collective-permute-start(bf16[4,2,32,512]{3,2,1,0:T(8,128)(2,1)S(1)} %get-tuple-element.13), channel_id=1, source_target_pairs={{0,16},{1,113},{2,18},{3,115},{4,20},{5,117},{6,22},{7,119},{8,24}... | collective-permute-start | bytes 786440 | tf_op jit(solution)/shard_map/ppermute | solution.py:355
  41.0 5.7 %collective-permute-done.got_ref = bf16[4,2,32,512]{3,2,1,0:T(8,128)(2,1)S(1)} collective-permute-done((bf16[4,2,32,512]{3,2,1,0:T(8,128)(2,1)S(1)}, bf16[4,2,32,512]{3,2,1,0:T(8,128)(2,1)S(1)}, u32[]{:S(2)}, u32[]{:S(2)}) %collective-permute-start) | collective-permute-done | bytes 262176 | tf_op jit(solution)/shard_map/ppermute | solution.py:355
  46.7 9.4 %collective-permute-start.1 = (bf16[2,32,512]{2,1,0:T(8,128)(2,1)S(1)}, bf16[2,32,512]{2,1,0:T(8,128)(2,1)S(1)}, u32[]{:S(2)}, u32[]{:S(2)}) collective-permute-start(bf16[2,32,512]{2,1,0:T(8,128)(2,1)S(1)} %get-tuple-element.15), channel_id=1, source_target_pairs={{0,64},{8,72},{16,80},{24,88},{32,96},{40,104},{48,112},{56,120},{... | collective-permute-start | bytes 196616 | tf_op jit(solution)/shard_map/ppermute | solution.py:368
  56.1 4.8 %collective-permute-start.2 = (bf16[2,32,512]{2,1,0:T(8,128)(2,1)S(1)}, bf16[2,32,512]{2,1,0:T(8,128)(2,1)S(1)}, u32[]{:S(2)}, u32[]{:S(2)}) collective-permute-start(bf16[2,32,512]{2,1,0:T(8,128)(2,1)S(1)} %get-tuple-element.16), channel_id=1, source_target_pairs={{0,32},{8,40},{16,48},{24,56},{32,64},{40,72},{48,80},{56,88},{64,... | collective-permute-start | bytes 196616 | tf_op jit(solution)/shard_map/ppermute | solution.py:368
  61.0 4.4 %collective-permute-start.3 = (bf16[2,32,512]{2,1,0:T(8,128)(2,1)S(1)}, bf16[2,32,512]{2,1,0:T(8,128)(2,1)S(1)}, u32[]{:S(2)}, u32[]{:S(2)}) collective-permute-start(bf16[2,32,512]{2,1,0:T(8,128)(2,1)S(1)} %get-tuple-element.17), channel_id=1, source_target_pairs={{0,96},{8,104},{16,112},{24,120},{32,0},{40,8},{48,16},{56,24},{64... | collective-permute-start | bytes 196616 | tf_op jit(solution)/shard_map/ppermute | solution.py:368
  65.3 0.0 collective-permute-done.1.refs_0_
  65.4 0.1 collective-permute-done.2.refs_1_
  65.5 9.5 %collective-permute-done.3.refs_2_ = bf16[2,32,512]{2,1,0:T(8,128)(2,1)S(1)} collective-permute-done((bf16[2,32,512]{2,1,0:T(8,128)(2,1)S(1)}, bf16[2,32,512]{2,1,0:T(8,128)(2,1)S(1)}, u32[]{:S(2)}, u32[]{:S(2)}) %collective-permute-start.3) | collective-permute-done | bytes 65568 | tf_op jit(solution)/shard_map/ppermute | solution.py:368
  75.1 7.2 %all_to_all.11.parts_ref = bf16[4,32,512]{2,1,0:T(8,128)(2,1)S(1)} all-to-all(bf16[4,32,512]{2,1,0:T(8,128)(2,1)S(1)} %get-tuple-element.19), channel_id=1, replica_groups=mesh['band'=4,'group'=16,'patch'=8] {'band'}, dimensions={0} | all-to-all | bytes 262144 | tf_op jit(solution)/shard_map/all_to_all | solution.py:380
  82.3 0.7 chi_sum.1
  (3 shorter events, 0.1 us)
Async XLA Ops:
  33.4 13.3 %collective-permute-start = (bf16[4,2,32,512]{3,2,1,0:T(8,128)(2,1)S(1)}, bf16[4,2,32,512]{3,2,1,0:T(8,128)(2,1)S(1)}, u32[]{:S(2)}, u32[]{:S(2)}) collective-permute-start(bf16[4,2,32,512]{3,2,1,0:T(8,128)(2,1)S(1)} %get-tuple-element.13), channel_id=1, source_target_pairs={{0,16},{1,113},{2,18},{3,115},{4,20},{5,117},{6,22},{7,119},{8,24}... | collective-permute-start | bytes 786440 | tf_op jit(solution)/shard_map/ppermute | solution.py:355
  46.7 18.6 %collective-permute-start.1 = (bf16[2,32,512]{2,1,0:T(8,128)(2,1)S(1)}, bf16[2,32,512]{2,1,0:T(8,128)(2,1)S(1)}, u32[]{:S(2)}, u32[]{:S(2)}) collective-permute-start(bf16[2,32,512]{2,1,0:T(8,128)(2,1)S(1)} %get-tuple-element.15), channel_id=1, source_target_pairs={{0,64},{8,72},{16,80},{24,88},{32,96},{40,104},{48,112},{56,120},{... | collective-permute-start | bytes 196616 | tf_op jit(solution)/shard_map/ppermute | solution.py:368
  56.1 9.4 %collective-permute-start.2 = (bf16[2,32,512]{2,1,0:T(8,128)(2,1)S(1)}, bf16[2,32,512]{2,1,0:T(8,128)(2,1)S(1)}, u32[]{:S(2)}, u32[]{:S(2)}) collective-permute-start(bf16[2,32,512]{2,1,0:T(8,128)(2,1)S(1)} %get-tuple-element.16), channel_id=1, source_target_pairs={{0,32},{8,40},{16,48},{24,56},{32,64},{40,72},{48,80},{56,88},{64,... | collective-permute-start | bytes 196616 | tf_op jit(solution)/shard_map/ppermute | solution.py:368
  61.0 14.1 %collective-permute-start.3 = (bf16[2,32,512]{2,1,0:T(8,128)(2,1)S(1)}, bf16[2,32,512]{2,1,0:T(8,128)(2,1)S(1)}, u32[]{:S(2)}, u32[]{:S(2)}) collective-permute-start(bf16[2,32,512]{2,1,0:T(8,128)(2,1)S(1)} %get-tuple-element.17), channel_id=1, source_target_pairs={{0,96},{8,104},{16,112},{24,120},{32,0},{40,8},{48,16},{56,24},{64... | collective-permute-start | bytes 196616 | tf_op jit(solution)/shard_map/ppermute | solution.py:368

commit v7 on v6

--- a/solution.py
+++ b/solution.py
@@ -120,7 +120,7 @@
     for copy in copies:
         copy.start()
     metas[...] = jnp.zeros_like(metas)
-    line = lax.broadcasted_iota(jnp.int32, (META_ROWS, TILE), 0)
+    line = lax.broadcasted_iota(jnp.int32, (META_ROWS, TILE), 1)
     for copy in copies[:3]:
         copy.wait()
     coef_full[...] = coef_half[...].astype(F32)
@@ -334,7 +334,7 @@
     slots_got = lax.all_to_all(
         slots, ("group", "patch"), 0, 0, tiled=True, axis_index_groups=blocks
     )
-    meta = slots_got[:, SLOT_ROWS : SLOT_ROWS + 8, 0].astype(jnp.int32)
+    meta = slots_got[:, SLOT_ROWS, :8].astype(jnp.int32)
     with jax.named_scope("strip_images"):
         kept, sent = pl.pallas_call(
             scatter_kernel,

time: 83.3 us -> 83.2 us (level)
  no operation moved by 1% of the time
where the time goes in v7:
time: 83.2 us; the launch traced here: 82.8 us
  blocking collectives  34.5 us (41%)
  starting transfers between devices  26.2 us (31%)
  waiting for transfers between devices  15.4 us (19%)
  Pallas kernels  6.03 us (7%)
    all_to_all x1, blocking collectives, on_device(): lax.all_to_all(slots, ('group', 'patch'), 0, 0, tiled=True, axis_index_gr...  27.3 us
    ppermute x3, starting transfers between devices, on_device(): strips_got.append(lax.ppermute(quads[step], 'group', ring))  18.6 us
    ppermute x3, waiting for transfers between devices, on_device(): strips_got.append(lax.ppermute(quads[step], 'group', ring))  9.7 us
    ppermute x1, starting transfers between devices, on_device(): got = lax.ppermute(sent, ('group', 'patch'), pairs)  7.59 us
    all_to_all x1, blocking collectives, on_device(): chi_parts = lax.all_to_all(chi_copies, 'band', 0, 0, tiled=True)  7.22 us
    ppermute x1, waiting for transfers between devices, on_device(): got = lax.ppermute(sent, ('group', 'patch'), pairs)  5.66 us
    pallas_call x1, Pallas kernels, on_device(): pl.pallas_call(slot_kernel, out_shape=jax.ShapeDtypeStruct((2, PATCHES, S...  3.98 us
  transfers between devices with their start and end apart: 4, of which 3 were waited for; matrix products, arithmetic and copies ran while one was open for 0% of the time, Pallas kernels for 0%

profile of v7, /device:TPU:1, one launch (start us, length us, event | category | flops | bytes accessed | tf_op | source)
XLA Modules:
  0.0 82.8 jit_solution(8248392014749923734)
XLA Ops:
  0.6 4.0 %tile_slots.1 = bf16[2,8,272,128]{3,2,1,0:T(8,128)(2,1)} custom-call(s32[1,8]{1,0:T(1,128)} %bitcast.21, s32[2,8]{1,0:T(2,128)} %bitcast.20, s32[4,8]{1,0:T(4,128)} %bitcast.18, bf16[8,27]{1,0:T(8,128)(2,1)} %bitcast.19, bf16[8,128,128]{2,1,0:T(8,128)(2,1)} %bitcast.16, bf16[8,128,128]{2,1,0:T(8,128)(2,1)} %bitcast.17, ...), custom_call_target="tpu_custom_call" | custom-call | tf_op jit(solution)/shard_map/tile_slots/pallas_call | solution.py:294
  4.6 27.3 %all_to_all.10.slots_ref = bf16[16,272,128]{2,1,0:T(8,128)(2,1)S(1)} all-to-all(bf16[16,272,128]{2,1,0:T(8,128)(2,1)} %bitcast.15), channel_id=1, replica_groups={{0,1,2,3,4,5,6,7,8,9,10,11,12,13,14,15},{16,17,18,19,20,21,22,23,24,25,..., dimensions={0} | all-to-all | bytes 2228224 | tf_op jit(solution)/shard_map/all_to_all | solution.py:334
  31.9 1.3 %strip_images.1 = (f32[4,2,32,512]{3,2,1,0:T(8,128)S(1)}, bf16[4,2,32,512]{3,2,1,0:T(8,128)(2,1)S(1)}) custom-call(s32[16,8]{1,0:T(8,128)S(1)} %bitcast.14, bf16[16,272,128]{2,1,0:T(8,128)(2,1)S(1)} %all_to_all.10.slots_ref), custom_call_target="tpu_custom_call" | custom-call | tf_op jit(solution)/shard_map/strip_images/pallas_call | solution.py:339
  33.2 7.6 %collective-permute-start = (bf16[4,2,32,512]{3,2,1,0:T(8,128)(2,1)S(1)}, bf16[4,2,32,512]{3,2,1,0:T(8,128)(2,1)S(1)}, u32[]{:S(2)}, u32[]{:S(2)}) collective-permute-start(bf16[4,2,32,512]{3,2,1,0:T(8,128)(2,1)S(1)} %get-tuple-element.13), channel_id=1, source_target_pairs={{0,16},{1,113},{2,18},{3,115},{4,20},{5,117},{6,22},{7,119},{8,24}... | collective-permute-start | bytes 786440 | tf_op jit(solution)/shard_map/ppermute | solution.py:355
  40.8 5.7 %collective-permute-done.got_ref = bf16[4,2,32,512]{3,2,1,0:T(8,128)(2,1)S(1)} collective-permute-done((bf16[4,2,32,512]{3,2,1,0:T(8,128)(2,1)S(1)}, bf16[4,2,32,512]{3,2,1,0:T(8,128)(2,1)S(1)}, u32[]{:S(2)}, u32[]{:S(2)}) %collective-permute-start) | collective-permute-done | bytes 262176 | tf_op jit(solution)/shard_map/ppermute | solution.py:355
  46.5 9.4 %collective-permute-start.1 = (bf16[2,32,512]{2,1,0:T(8,128)(2,1)S(1)}, bf16[2,32,512]{2,1,0:T(8,128)(2,1)S(1)}, u32[]{:S(2)}, u32[]{:S(2)}) collective-permute-start(bf16[2,32,512]{2,1,0:T(8,128)(2,1)S(1)} %get-tuple-element.15), channel_id=1, source_target_pairs={{0,64},{8,72},{16,80},{24,88},{32,96},{40,104},{48,112},{56,120},{... | collective-permute-start | bytes 196616 | tf_op jit(solution)/shard_map/ppermute | solution.py:368
  56.0 4.8 %collective-permute-start.2 = (bf16[2,32,512]{2,1,0:T(8,128)(2,1)S(1)}, bf16[2,32,512]{2,1,0:T(8,128)(2,1)S(1)}, u32[]{:S(2)}, u32[]{:S(2)}) collective-permute-start(bf16[2,32,512]{2,1,0:T(8,128)(2,1)S(1)} %get-tuple-element.16), channel_id=1, source_target_pairs={{0,32},{8,40},{16,48},{24,56},{32,64},{40,72},{48,80},{56,88},{64,... | collective-permute-start | bytes 196616 | tf_op jit(solution)/shard_map/ppermute | solution.py:368
  60.8 4.4 %collective-permute-start.3 = (bf16[2,32,512]{2,1,0:T(8,128)(2,1)S(1)}, bf16[2,32,512]{2,1,0:T(8,128)(2,1)S(1)}, u32[]{:S(2)}, u32[]{:S(2)}) collective-permute-start(bf16[2,32,512]{2,1,0:T(8,128)(2,1)S(1)} %get-tuple-element.17), channel_id=1, source_target_pairs={{0,96},{8,104},{16,112},{24,120},{32,0},{40,8},{48,16},{56,24},{64... | collective-permute-start | bytes 196616 | tf_op jit(solution)/shard_map/ppermute | solution.py:368
  65.2 0.0 collective-permute-done.1.refs_0_
  65.2 0.2 collective-permute-done.2.refs_1_
  65.3 9.5 %collective-permute-done.3.refs_2_ = bf16[2,32,512]{2,1,0:T(8,128)(2,1)S(1)} collective-permute-done((bf16[2,32,512]{2,1,0:T(8,128)(2,1)S(1)}, bf16[2,32,512]{2,1,0:T(8,128)(2,1)S(1)}, u32[]{:S(2)}, u32[]{:S(2)}) %collective-permute-start.3) | collective-permute-done | bytes 65568 | tf_op jit(solution)/shard_map/ppermute | solution.py:368
  74.9 7.2 %all_to_all.11.parts_ref = bf16[4,32,512]{2,1,0:T(8,128)(2,1)S(1)} all-to-all(bf16[4,32,512]{2,1,0:T(8,128)(2,1)S(1)} %get-tuple-element.19), channel_id=1, replica_groups=mesh['band'=4,'group'=16,'patch'=8] {'band'}, dimensions={0} | all-to-all | bytes 262144 | tf_op jit(solution)/shard_map/all_to_all | solution.py:380
  82.1 0.7 chi_sum.1
  (3 shorter events, 0.1 us)
Async XLA Ops:
  33.2 13.3 %collective-permute-start = (bf16[4,2,32,512]{3,2,1,0:T(8,128)(2,1)S(1)}, bf16[4,2,32,512]{3,2,1,0:T(8,128)(2,1)S(1)}, u32[]{:S(2)}, u32[]{:S(2)}) collective-permute-start(bf16[4,2,32,512]{3,2,1,0:T(8,128)(2,1)S(1)} %get-tuple-element.13), channel_id=1, source_target_pairs={{0,16},{1,113},{2,18},{3,115},{4,20},{5,117},{6,22},{7,119},{8,24}... | collective-permute-start | bytes 786440 | tf_op jit(solution)/shard_map/ppermute | solution.py:355
  46.5 18.6 %collective-permute-start.1 = (bf16[2,32,512]{2,1,0:T(8,128)(2,1)S(1)}, bf16[2,32,512]{2,1,0:T(8,128)(2,1)S(1)}, u32[]{:S(2)}, u32[]{:S(2)}) collective-permute-start(bf16[2,32,512]{2,1,0:T(8,128)(2,1)S(1)} %get-tuple-element.15), channel_id=1, source_target_pairs={{0,64},{8,72},{16,80},{24,88},{32,96},{40,104},{48,112},{56,120},{... | collective-permute-start | bytes 196616 | tf_op jit(solution)/shard_map/ppermute | solution.py:368
  56.0 9.4 %collective-permute-start.2 = (bf16[2,32,512]{2,1,0:T(8,128)(2,1)S(1)}, bf16[2,32,512]{2,1,0:T(8,128)(2,1)S(1)}, u32[]{:S(2)}, u32[]{:S(2)}) collective-permute-start(bf16[2,32,512]{2,1,0:T(8,128)(2,1)S(1)} %get-tuple-element.16), channel_id=1, source_target_pairs={{0,32},{8,40},{16,48},{24,56},{32,64},{40,72},{48,80},{56,88},{64,... | collective-permute-start | bytes 196616 | tf_op jit(solution)/shard_map/ppermute | solution.py:368
  60.8 14.1 %collective-permute-start.3 = (bf16[2,32,512]{2,1,0:T(8,128)(2,1)S(1)}, bf16[2,32,512]{2,1,0:T(8,128)(2,1)S(1)}, u32[]{:S(2)}, u32[]{:S(2)}) collective-permute-start(bf16[2,32,512]{2,1,0:T(8,128)(2,1)S(1)} %get-tuple-element.17), channel_id=1, source_target_pairs={{0,96},{8,104},{16,112},{24,120},{32,0},{40,8},{48,16},{56,24},{64... | collective-permute-start | bytes 196616 | tf_op jit(solution)/shard_map/ppermute | solution.py:368
